TPU v7x, 256 devices: a whole 4x4x8 slice. The times are simulated.
256 devices in a mesh: lon: 128 (over y, z, x_hi, core), tm: 2 (over x_lo).
Axes of the slice: x: 4 (x_hi: 2, x_lo: 2; x = x_hi * 2 + x_lo), y: 4, z: 8, core: 2. Of those that a mesh axis runs over, the one named last changes fastest.
Arguments:
- video: bfloat16 [8, 8, 1024, 384], P('tm', None, 'lon'), may hold values from -6 to 6
- gain_one: float32 [384], replicated, may hold values from 0.1 to 1.9
- weight_one: bfloat16 [27, 384, 384], P(None, 'lon'), may hold values from -0.0625 to 0.0625
- bias_one: float32 [384], replicated, may hold values from -3 to 3
- gain_two: float32 [384], replicated, may hold values from 0.1 to 1.9
- weight_two: bfloat16 [27, 384, 384], P(None, 'lon'), may hold values from -0.0625 to 0.0625
- bias_two: float32 [384], replicated, may hold values from -2 to 2
- cache_one: bfloat16 [2, 8, 1024, 384], P(None, None, 'lon'), may hold values from -6 to 6
- cache_two: bfloat16 [2, 8, 1024, 384], P(None, None, 'lon'), may hold values from -6 to 6
Outputs:
- result: bfloat16 [8, 8, 1024, 384], P('tm', None, 'lon')
All inputs are finite; a program needn't handle non-finite values.
Results may differ from a plain program's by a relative error of at most 0.0033.
Values may be sent and summed in bfloat16 or wider, within the bound.
No kernel may reach another device: no remote copies, remote signals or barrier semaphores. Data moves between devices by JAX's collectives and lax.ppermute only.
A program may use at most 128 MiB of HBM per device.

v0:
```python
import jax
import jax.numpy as jnp
from jax import lax
from jax.sharding import PartitionSpec as P


def passed_along(block, axis, distance):
    devices = range(lax.axis_size(axis))
    route = [(i - distance, i) for i in devices if i - distance in devices]
    return lax.ppermute(block, axis, route)


def with_halo(value, sides, width):
    for axis, dim in sides:
        count, length = (lax.axis_size(axis), value.shape[dim])
        up = [(i, (i + 1) % count) for i in range(count)]
        down = [(j, i) for i, j in up]
        last = lax.slice_in_dim(value, length - width, length, axis=dim)
        leading = lax.slice_in_dim(value, 0, width, axis=dim)
        before = lax.ppermute(last, axis, up)
        after = lax.ppermute(leading, axis, down)
        value = jnp.concatenate([before, value, after], axis=dim)
    return value


def norm_silu(values, gain):
    square = jnp.mean(values * values, axis=-1, keepdims=True)
    scaled = values * lax.rsqrt(square + 1e-06) * gain
    return jax.nn.silu(scaled).astype(jnp.bfloat16)


def pad_rows(field):
    return jnp.pad(field, ((0, 0), (1, 1), (0, 0), (0, 0)))


def tap_terms(padded, total, piece):
    frames_out = padded.shape[0] - 2
    lat_rows = padded.shape[1] - 2
    columns = padded.shape[2] - 2
    width = piece.shape[1]
    for frame_tap in range(3):
        for row_tap in range(3):
            for column_tap in range(3):
                window = padded[
                    frame_tap : frame_tap + frames_out,
                    row_tap : row_tap + lat_rows,
                    column_tap : column_tap + columns,
                ]
                kernel = piece[9 * frame_tap + 3 * row_tap + column_tap]
                total = total + jnp.dot(
                    window.reshape(-1, width), kernel, preferred_element_type=jnp.float32
                )
    return total


def empty_sum(padded, channels):
    rows_out = (padded.shape[0] - 2) * (padded.shape[1] - 2) * (padded.shape[2] - 2)
    return jnp.zeros((rows_out, channels), jnp.float32)


def finish(total, padded, offset):
    return total.reshape(padded.shape[0] - 2, padded.shape[1] - 2, padded.shape[2] - 2, -1) + offset


def per_device(
    video, gain_one, weight_one, bias_one, gain_two, weight_two, bias_two, cache_one, cache_two
):
    leading = lax.axis_index("tm") == 0
    frame_count = video.shape[0]
    channels = weight_one.shape[2]
    first_in = norm_silu(video.astype(jnp.float32), gain_one)
    earlier = passed_along(first_in[frame_count - 2 :], "tm", 1)
    extended = jnp.concatenate([jnp.where(leading, cache_one, earlier), first_in], axis=0)
    padded_one = pad_rows(with_halo(extended, (("lon", 2),), 1))
    total_one = tap_terms(
        padded_one,
        empty_sum(padded_one, channels),
        lax.all_gather(weight_one, "lon", axis=1, tiled=True),
    )
    hidden = finish(total_one, padded_one, bias_one)
    second_all = norm_silu(hidden, gain_two)
    later = passed_along(second_all[frame_count - 2 :], "tm", 1)
    second_ext = jnp.concatenate([jnp.where(leading, cache_two, later), second_all], axis=0)
    padded_two = pad_rows(with_halo(second_ext, (("lon", 2),), 1))
    total_two = tap_terms(
        padded_two,
        empty_sum(padded_two, channels),
        lax.all_gather(weight_two, "lon", axis=1, tiled=True),
    )
    branch = finish(total_two, padded_two, bias_two)
    return (video.astype(jnp.float32) + branch).astype(jnp.bfloat16)


def solution(mesh):
    in_specs = (
        P("tm", None, "lon", None),
        P(),
        P(None, "lon", None),
        P(),
        P(),
        P(None, "lon", None),
        P(),
        P(None, None, "lon", None),
        P(None, None, "lon", None),
    )
    out_specs = P("tm", None, "lon", None)
    return jax.shard_map(
        per_device, mesh=mesh, in_specs=in_specs, out_specs=out_specs, check_vma=False
    )
```

profile of v0, /device:TPU:1, one launch (start us, length us, event | category | flops | bytes accessed | tf_op | source)
XLA Modules:
  0.0 331.6 jit_solution(9906638441270217489)
XLA Ops:
  6.5 0.7 all-gather.3.cloned.1.call-update
  8.0 1.0 fusion.11
  9.1 1.1 fusion.18
  10.2 4.0 %collective-permute-start = (bf16[2,8,8,384]{3,2,1,0:T(8,128)(2,1)S(1)}, bf16[2,8,8,384]{3,2,1,0:T(8,128)(2,1)S(1)}, u32[]{:S(2)}, u32[]{:S(2)}) collective-permute-start(bf16[2,8,8,384]{3,2,1,0:T(8,128)(2,1)S(1)} %slice.486), channel_id=1, source_target_pairs={{0,1},{2,3},{4,5},{6,7},{8,9},{10,11},{12,13},{14,15},{16,17},{18,... | collective-permute-start | bytes 294920 | tf_op jit(solution)/shard_map/ppermute | solution.py:10
  14.2 1.6 collective-permute-done
  15.8 0.9 broadcast_select_fusion.1
  16.9 3.9 %collective-permute-start.1 = (bf16[6,8,1,384]{3,2,1,0:T(2,128)(2,1)S(1)}, bf16[6,8,1,384]{3,2,1,0:T(2,128)(2,1)S(1)}, u32[]{:S(2)}, u32[]{:S(2)}) collective-permute-start(bf16[6,8,1,384]{3,2,1,0:T(2,128)(2,1)S(1)} %get-tuple-element.117), channel_id=1, source_target_pairs={{0,2},{2,4},{4,6},{6,8},{8,10},{10,12},{12,14},{14,16},{16,18},{18... | collective-permute-start | bytes 110600 | tf_op jit(solution)/shard_map/ppermute | solution.py:20
  20.8 0.7 pad_maximum_fusion.3
  22.2 5.0 %collective-permute-done.2 = bf16[6,8,1,384]{3,2,1,0:T(2,128)(2,1)S(1)} collective-permute-done((bf16[6,8,1,384]{3,2,1,0:T(2,128)(2,1)S(1)}, bf16[6,8,1,384]{3,2,1,0:T(2,128)(2,1)S(1)}, u32[]{:S(2)}, u32[]{:S(2)}) %collective-permute-start.2) | collective-permute-done | bytes 36896 | tf_op jit(solution)/shard_map/ppermute | solution.py:21
  27.9 1.0 fusion.41
  28.9 1.6 fusion.38
  30.5 117.0 %all-gather.3.cloned.1.call-done = bf16[27,384,384]{2,0,1:T(8,128)(2,1)} async-done(((bf16[27,3,384]{2,0,1:T(8,128)(2,1)}), bf16[27,384,384]{2,0,1:T(8,128)(2,1)}) %all-gather.3.cloned.1.call-update) | async-done | bytes 7962640 | tf_op jit(solution)/shard_map/all_gather | solution.py:78
  147.5 11.2 %fusion.36 = (bf16[1,384,384]{2,0,1:T(2,128)(2,1)S(1)}, bf16[1,384,384]{2,0,1:T(2,128)(2,1)S(1)}, bf16[1,384,384]{2,0,1:T(2,128)(2,1)S(1)}, bf16[1,384,384]{2,0,...) fusion(bf16[27,384,384]{2,0,1:T(8,128)(2,1)} %all-gather.3.clon, ...), kind=kLoop, calls=%fused_computation.174 | loop fusion | bytes 4718592 | tf_op jit(solution)/shard_map/slice | solution.py:49
  161.0 10.7 %fusion.35 = (bf16[1,384,384]{2,0,1:T(2,128)(2,1)}, bf16[1,384,384]{2,0,1:T(2,128)(2,1)S(1)}, bf16[1,384,384]{2,0,1:T(2,128)(2,1)S(1)}, bf16[1,384,384]{2,0,1:T(...) fusion(bf16[27,384,384]{2,0,1:T(8,128)(2,1)S(1)} %bitcast.273), kind=kLoop, calls=%fused_computation.173 | loop fusion | bytes 11206656 | tf_op jit(solution)/shard_map/slice | solution.py:49
  171.8 1.4 convolution_add_fusion.44
  176.4 0.8 copy-done.8
  177.5 0.8 copy-done.7
  183.7 2.8 collective-permute-start.3
  186.5 93.6 %all-gather.5.cloned.1.call-done = bf16[27,384,384]{2,0,1:T(8,128)(2,1)} async-done(((bf16[27,3,384]{2,0,1:T(8,128)(2,1)}), bf16[27,384,384]{2,0,1:T(8,128)(2,1)}) %all-gather.5.cloned.1.call-update) | async-done | bytes 7962640 | tf_op jit(solution)/shard_map/all_gather | solution.py:88
  280.1 22.4 %fusion.33 = (bf16[1,384,384]{2,0,1:T(2,128)(2,1)S(1)}, bf16[1,384,384]{2,0,1:T(2,128)(2,1)S(1)}, bf16[1,384,384]{2,0,1:T(2,128)(2,1)S(1)}, bf16[1,384,384]{2,0,...) fusion(bf16[27,384,384]{2,0,1:T(8,128)(2,1)} %all-gather.5.clon, ...), kind=kLoop, calls=%fused_computation.171 | loop fusion | bytes 11206656 | tf_op jit(solution)/shard_map/slice | solution.py:49
  302.5 4.3 %fusion.34 = (bf16[1,384,384]{2,0,1:T(2,128)(2,1)S(1)}, bf16[1,384,384]{2,0,1:T(2,128)(2,1)S(1)}, bf16[1,384,384]{2,0,1:T(2,128)(2,1)S(1)}, bf16[1,384,384]{2,0,...) fusion(bf16[27,384,384]{2,0,1:T(8,128)(2,1)S(1)} %copy-done), kind=kLoop, calls=%fused_computation.172 | loop fusion | bytes 4718592 | tf_op jit(solution)/shard_map/slice | solution.py:49
  307.8 1.2 collective-permute-done.4
  309.0 3.9 %collective-permute-done.5 = bf16[6,8,1,384]{3,2,1,0:T(2,128)(2,1)S(1)} collective-permute-done((bf16[6,8,1,384]{3,2,1,0:T(2,128)(2,1)S(1)}, bf16[6,8,1,384]{3,2,1,0:T(2,128)(2,1)S(1)}, u32[]{:S(2)}, u32[]{:S(2)}) %collective-permute-start.5) | collective-permute-done | bytes 36896 | tf_op jit(solution)/shard_map/ppermute | solution.py:21
  324.0 0.7 fusion.19
  (155 shorter events, 24.9 us)
Async XLA Ops:
  6.5 140.9 %all-gather.3.cloned.1.call-start = ((), (), s32[]{:S(2)}) async-start(), calls=%async_computation | async-start | bytes 9510912 | tf_op jit(solution)/shard_map/all_gather | solution.py:78
  7.3 272.9 %all-gather.5.cloned.1.call-start = ((), (), s32[]{:S(2)}) async-start(), calls=%async_computation.1 | async-start | bytes 9510912 | tf_op jit(solution)/shard_map/all_gather | solution.py:88
  10.2 5.6 %collective-permute-start = (bf16[2,8,8,384]{3,2,1,0:T(8,128)(2,1)S(1)}, bf16[2,8,8,384]{3,2,1,0:T(8,128)(2,1)S(1)}, u32[]{:S(2)}, u32[]{:S(2)}) collective-permute-start(bf16[2,8,8,384]{3,2,1,0:T(8,128)(2,1)S(1)} %slice.486), channel_id=1, source_target_pairs={{0,1},{2,3},{4,5},{6,7},{8,9},{10,11},{12,13},{14,15},{16,17},{18,... | collective-permute-start | bytes 294920 | tf_op jit(solution)/shard_map/ppermute | solution.py:10
  16.9 5.4 %collective-permute-start.1 = (bf16[6,8,1,384]{3,2,1,0:T(2,128)(2,1)S(1)}, bf16[6,8,1,384]{3,2,1,0:T(2,128)(2,1)S(1)}, u32[]{:S(2)}, u32[]{:S(2)}) collective-permute-start(bf16[6,8,1,384]{3,2,1,0:T(2,128)(2,1)S(1)} %get-tuple-element.117), channel_id=1, source_target_pairs={{0,2},{2,4},{4,6},{6,8},{8,10},{10,12},{12,14},{14,16},{16,18},{18... | collective-permute-start | bytes 110600 | tf_op jit(solution)/shard_map/ppermute | solution.py:20
  20.8 6.4 %collective-permute-start.2 = (bf16[6,8,1,384]{3,2,1,0:T(2,128)(2,1)S(1)}, bf16[6,8,1,384]{3,2,1,0:T(2,128)(2,1)S(1)}, u32[]{:S(2)}, u32[]{:S(2)}) collective-permute-start(bf16[6,8,1,384]{3,2,1,0:T(2,128)(2,1)S(1)} %get-tuple-element.118), channel_id=1, source_target_pairs={{2,0},{4,2},{6,4},{8,6},{10,8},{12,10},{14,12},{16,14},{18,16},{20... | collective-permute-start | bytes 110600 | tf_op jit(solution)/shard_map/ppermute | solution.py:21
  147.5 13.5 %slice-start = ((s8[9437184]{0:T(1024)(128)(4,1)}), s8[4194304]{0:T(1024)(128)(4,1)S(1)}, s32[]{:S(2)}) async-start(s8[9437184]{0:T(1024)(128)(4,1)} %bitcast.272), calls=%async_computation.2 | async-start | bytes 8388608
  147.5 13.5 %slice-start.1 = ((s8[9437184]{0:T(1024)(128)(4,1)}), s8[4194304]{0:T(1024)(128)(4,1)S(1)}, s32[]{:S(2)}) async-start(s8[9437184]{0:T(1024)(128)(4,1)} %bitcast.272), calls=%async_computation.3 | async-start | bytes 8388608
  159.3 1.7 slice-start.2
  161.0 10.7 %copy-start.24 = (bf16[4,8,8,384]{3,2,1,0:T(8,128)(2,1)S(1)}, bf16[4,8,8,384]{3,2,1,0:T(8,128)(2,1)}, u32[]{:S(2)}) copy-start(bf16[4,8,8,384]{3,2,1,0:T(8,128)(2,1)} %get-tuple-element.89) | copy-start | bytes 589828
  161.0 12.2 %copy-start.23 = (bf16[4,8,8,384]{3,2,1,0:T(8,128)(2,1)S(1)}, bf16[4,8,8,384]{3,2,1,0:T(8,128)(2,1)}, u32[]{:S(2)}) copy-start(bf16[4,8,8,384]{3,2,1,0:T(8,128)(2,1)} %get-tuple-element.88) | copy-start | bytes 589828
  171.7 1.8 copy-start.13
  171.7 1.8 copy-start.22
  173.8 1.2 copy-start.10
  173.8 1.2 copy-start.30
  174.9 1.5 copy-start.20
  175.3 2.1 copy-start.19
  176.4 2.1 copy-start.18
  177.4 1.4 copy-start.17
  181.6 1.3 copy-start.34
  183.7 123.2 %collective-permute-start.3 = (bf16[2,8,8,384]{3,2,1,0:T(8,128)(2,1)}, bf16[2,8,8,384]{3,2,1,0:T(8,128)(2,1)}, u32[]{:S(2)}, u32[]{:S(2)}) collective-permute-start(bf16[2,8,8,384]{3,2,1,0:T(8,128)(2,1)} %slice.544), channel_id=1, source_target_pairs={{0,1},{2,3},{4,5},{6,7},{8,9},{10,11},{12,13},{14,15},{16,17},{18,... | collective-permute-start | bytes 294920 | tf_op jit(solution)/shard_map/ppermute | solution.py:10
  280.1 22.4 %copy-start = (bf16[27,384,384]{2,0,1:T(8,128)(2,1)S(1)}, bf16[27,384,384]{2,0,1:T(8,128)(2,1)}, u32[]{:S(2)}) copy-start(bf16[27,384,384]{2,0,1:T(8,128)(2,1)} %all-gather.5.cloned.1.call-done) | copy-start | bytes 23887876
  302.5 4.3 %copy-start.32 = (bf16[2,8,8,384]{3,2,1,0:T(8,128)(2,1)S(1)}, bf16[2,8,8,384]{3,2,1,0:T(8,128)(2,1)}, u32[]{:S(2)}) copy-start(bf16[2,8,8,384]{3,2,1,0:T(8,128)(2,1)} %param.17) | copy-start | bytes 294916
  307.1 1.9 collective-permute-start.4
  307.6 5.3 %collective-permute-start.5 = (bf16[6,8,1,384]{3,2,1,0:T(2,128)(2,1)S(1)}, bf16[6,8,1,384]{3,2,1,0:T(2,128)(2,1)S(1)}, u32[]{:S(2)}, u32[]{:S(2)}) collective-permute-start(bf16[6,8,1,384]{3,2,1,0:T(2,128)(2,1)S(1)} %get-tuple-element.112), channel_id=1, source_target_pairs={{2,0},{4,2},{6,4},{8,6},{10,8},{12,10},{14,12},{16,14},{18,16},{20... | collective-permute-start | bytes 110600 | tf_op jit(solution)/shard_map/ppermute | solution.py:21
  (23 other events, 24.2 us)
Sparse Core Ops, SparseCore 0:
  11.2 136.1 all-gather.2
  151.4 128.7 all-gather.4
where the time goes:
time: 335 us; the launch traced here: 332 us
  waiting for transfers between devices  224 us (67%)
  local copies, waits for them, and re-layouts  59 us (18%)
  matrix products  16.1 us (5%)
  between operations  14.3 us (4%)
  starting transfers between devices  11.4 us (3%)
  other arithmetic  6.51 us (2%)
    all_gather x1, waiting for transfers between devices, per_device(): lax.all_gather(weight_one, 'lon', axis=1, tiled=True)  117 us
    all_gather x1, waiting for transfers between devices, per_device(): lax.all_gather(weight_two, 'lon', axis=1, tiled=True)  93.6 us
    slice x4, local copies, waits for them, and re-layouts, tap_terms(): kernel = piece[9 * frame_tap + 3 * row_tap + column_tap]  48.6 us
    dot_general x54, matrix products, tap_terms(): jnp.dot(window.reshape(-1, width), kernel, preferred_element_type=jnp.flo...  16.1 us
    ppermute x2, waiting for transfers between devices, with_halo(): after = lax.ppermute(leading, axis, down)  8.83 us
    ppermute x2, starting transfers between devices, passed_along(): return lax.ppermute(block, axis, route)  6.79 us
  transfers between devices with their start and end apart: 8, of which 7 were waited for; matrix products, arithmetic and copies ran while one was open for 20% of the time, Pallas kernels for 0%

commit v1 on v0

v1 whole, which is shorter than its diff:
```python
import jax
import jax.numpy as jnp
from jax import lax
from jax.experimental import pallas as pl
from jax.experimental.pallas import tpu as pltpu
from jax.sharding import Mesh
from jax.sharding import PartitionSpec as P

LON = ("y", "z", "xh", "core")
RING = ("xh", "core", "tm")
PLANE = ("y", "z")
F32 = jnp.float32
BF16 = jnp.bfloat16
MIB = 1 << 20


def lanes(shape):
    return lax.broadcasted_iota(jnp.int32, shape, len(shape) - 1)


def half_roll(x):
    return pltpu.roll(x, 64, x.ndim - 1)


def norm_silu(x, gain):
    square = jnp.mean(x * x, axis=-1, keepdims=True)
    scaled = x * lax.rsqrt(square + 1e-06) * gain
    return scaled / (1.0 + jnp.exp(-scaled))


def put(wide, at, value):
    for k in range(3):
        wide[k, at : at + value.shape[0]] = value[:, 128 * k : 128 * k + 128]


def every(wide, start, step):
    return jnp.concatenate([wide[k, pl.ds(start, 8, stride=step), :] for k in range(3)], axis=1)


def spread_matrix():
    row = lax.broadcasted_iota(jnp.int32, (384, 512), 0)
    k = lax.broadcasted_iota(jnp.int32, (384, 512), 1)
    q, r, yz = k >> 7, (k >> 5) & 3, k & 31
    return jnp.where((row == 12 * yz + 3 * q + r) & (r < 3), 1.0, 0.0)


def order_matrix():
    row = lax.broadcasted_iota(jnp.int32, (384, 384), 0)
    k = lax.broadcasted_iota(jnp.int32, (384, 384), 1)
    r, z, y, q = k >> 7, (k >> 4) & 7, (k >> 2) & 3, k & 3
    return jnp.where(row == 96 * y + 12 * z + 3 * q + r, 1.0, 0.0)


def pack(slot, taps, half):
    first = half == 0
    low_lanes = lanes((14, 128)) < 64
    for r, w in enumerate(taps):
        slot[pl.ds(r, 27, stride=3), :] = jnp.where(first, w[:, :128], w[:, 128:256])
        rest = w[:, 256:]
        turned = half_roll(rest)
        low = jnp.where(first, rest, turned)[:14]
        high = jnp.concatenate([jnp.where(first, turned, rest)[14:], jnp.zeros((1, 128), F32)], axis=0)
        slot[pl.ds(81 + r, 14, stride=3), :] = jnp.where(low_lanes, low, high)
    slot[123:] = jnp.zeros((5, 128), F32)


def send_kernel(ids, w1, w2, video, cache1, cache2, out1, out2, out_edge, slot, wide, edge):
    taps2 = [w2[r].astype(F32) for r in range(3)]
    for half in range(2):
        pack(slot, taps2, half)
        packed = slot[...].astype(BF16)
        for n in range(8):
            out2[2 * n + half] = packed
    order = order_matrix().astype(BF16)
    taps1 = [jnp.dot(w1[r], order, preferred_element_type=F32) for r in range(3)]
    pack(slot, taps1, ids[1])
    packed = slot[:124].astype(BF16)
    for n in range(8):
        out1[n] = packed

    upper = ids[0] == 1
    put(wide, 0, video[...].astype(F32).reshape(256, 384))
    put(wide, 256, cache1[ids[1]].astype(F32).reshape(64, 384))
    put(wide, 320, cache2[...].astype(F32).reshape(128, 384))

    def column(f, low, high):
        return jnp.where(upper, every(wide, 64 * f + high, 8), every(wide, 64 * f + low, 8))

    for c in range(2):
        for f in range(5):
            at = 40 * c + 8 * f
            edge[at : at + 8] = column(f, c, 6 + c)
    for f in range(2):
        edge[80 + 8 * f : 88 + 8 * f] = column(5 + f, 0, 7)
    out_edge[...] = edge[...].astype(BF16)


def turn_kernel(x, out, wide):
    wide[...] = x[...].astype(F32).reshape(2048, 128)

    def step(row, carry):
        out[row] = wide[pl.ds(row, 16, stride=128), :].astype(BF16)
        return carry

    lax.fori_loop(0, 128, step, 0, unroll=8)


def by_slice(x, gain):
    frame = lax.rem(lax.broadcasted_iota(jnp.int32, x.shape, 0) >> 3, 5)
    x = jnp.where(frame == 4, x, norm_silu(x, gain)).astype(BF16)
    return jnp.dot(x, spread_matrix().astype(BF16), preferred_element_type=F32).astype(BF16)


def ordered(x):
    return jnp.dot(x.astype(BF16), order_matrix().astype(BF16), preferred_element_type=F32).astype(BF16)


def own_kernel(ids, video, cache1, cache2, gain1, bias1, gain2, out, out_cache, out_vec, wide, rows):
    put(wide, 0, video[...].astype(F32).reshape(256, 384))
    put(wide, 256, cache1[ids[1]].astype(F32).reshape(64, 384))
    put(wide, 320, cache2[...].astype(F32).reshape(128, 384))
    for c in range(8):
        for f in range(5):
            at = 40 * c + 8 * f
            rows[at : at + 8] = every(wide, 64 * f + c, 8)
    slices = by_slice(rows[...], gain1[...].reshape(1, 384))
    for q in range(4):
        out[q] = slices[:, 128 * q : 128 * q + 128]
    for c in range(8):
        for f in range(2):
            at = 16 * c + 8 * f
            rows[at : at + 8] = every(wide, 320 + 64 * f + c, 8)
    out_cache[...] = ordered(rows[0:128]).reshape(8, 16, 384)
    vectors = jnp.concatenate(
        [bias1[...].reshape(1, 384), gain2[...].reshape(1, 384), gain1[...].reshape(1, 384), jnp.zeros((5, 384), F32)],
        axis=0,
    )
    placed = jnp.dot(vectors, order_matrix(), preferred_element_type=F32, precision=lax.Precision.HIGHEST)
    out_vec[...] = jnp.concatenate([placed[:2], vectors[2:]], axis=0)


def enter_kernel(ids, own, cache, vec, halo, out, out_cache):
    slices = by_slice(halo[0:80].astype(F32), vec[2:3])
    for q in range(4):
        for tm in range(2):
            out[2 * q + tm, 0:320] = own[q]
            out[2 * q + tm, 320:400] = slices[:, 128 * q : 128 * q + 128]
    beyond = ordered(halo[80:96])

    @pl.when(ids[0] == 0)
    def _():
        out_cache[0] = beyond
        out_cache[1:9] = cache[...]

    @pl.when(ids[0] == 1)
    def _():
        out_cache[0:8] = cache[...]
        out_cache[8] = beyond


def shifted_rows(x, p):
    if p == 1:
        return x
    axis = x.ndim - 2
    lat = lax.broadcasted_iota(jnp.int32, x.shape, axis)
    if p == 0:
        return jnp.where(lat == 0, 0.0, pltpu.roll(x, 1, axis))
    return jnp.where(lat == 7, 0.0, pltpu.roll(x, 7, axis))


def tap_of(t):
    return t // 9, (t // 3) % 3, t % 3


def first_kernel(ids, x, w0, w1, w2, w3, out_own, out_peer, field, even, odd, wide, kernel, part_a, part_b):
    for s in range(8):
        q, tm = s // 2, s % 2
        piece = x[s].astype(F32).reshape(10, 5, 8, 128)
        places = [(2 + 8 * q, 0, 8)]
        if q == 0:
            places.append((0, 8, 10))
        if q == 3:
            places.append((34, 8, 10))
        for at, begin, end in places:
            n = end - begin
            field[at : at + n, 2 + 4 * tm : 6 + 4 * tm] = piece[begin:end, 0:4]
            field[at : at + n, tm] = piece[begin:end, 4]

    def spread(c, carry):
        plane = field[c]
        for p in range(3):
            moved = shifted_rows(plane, p)
            even[p, c] = moved.reshape(80, 128).astype(BF16)
            odd[p, c] = moved[1:9].reshape(64, 128).astype(BF16)
        return carry

    lax.fori_loop(0, 36, spread, 0, unroll=4)

    for d, w in enumerate((w0, w1, w2, w3)):
        at = pl.multiple_of(1024 * ((ids[3] + 4 - d) & 3), 1024)
        for z in range(8):
            wide[pl.ds(at + 128 * z, 124), :] = w[z].astype(F32)
    for t in range(27):
        for r in range(3):
            kernel[t, 32 * r : 32 * r + 32, 0:128] = wide[pl.ds(3 * t + r, 32, stride=128), :].astype(BF16)
            kernel[t, 32 * r : 32 * r + 32, 128:256] = wide[
                pl.ds(81 + 3 * (t % 14) + r, 32, stride=128), :
            ].astype(BF16)
        kernel[t, 96:128] = jnp.zeros((32, 256), BF16)

    block = 34

    def multiply(i, carry):
        at = i * block

        def window(t):
            a, p, q = tap_of(t)
            if a == 1:
                rows = odd[p, pl.ds(at + q, block)]
            else:
                rows = even[p, pl.ds(at + q, block), 8 * a : 8 * a + 64]
            return rows.reshape(block * 64, 128)

        def total(taps):
            left = jnp.concatenate([window(t) for t in taps], axis=1)
            right = kernel[taps[0] : taps[-1] + 1].reshape(128 * len(taps), 256)
            return jnp.dot(left, right, preferred_element_type=F32)

        low = total(range(0, 14))
        high = total(range(14, 27))
        part_a[pl.ds(at, block)] = (low[:, :128] + high[:, :128]).reshape(block, 64, 128)
        part_b[pl.ds(at, block)] = (low[:, 128:] + half_roll(high[:, 128:])).reshape(block, 64, 128)
        return carry

    lax.fori_loop(0, 34 // block, multiply, 0)

    low_lanes = lanes((48, 128)) < 64
    for d in range(4):
        xh, tm = d // 2, d % 2
        for out, core in ((out_own, ids[0]), (out_peer, 1 - ids[0])):
            base = 16 * xh + 9 * core

            def rows_of(part, c):
                if tm == 1:
                    return part[c, 16:64]
                return jnp.concatenate([jnp.zeros((16, 128), F32), part[c, 0:32]], axis=0)

            for j in range(9):
                out[d, j] = rows_of(part_a, base + j).astype(BF16)
            for j in range(5):
                b = rows_of(part_b, base + j)
                if j < 4:
                    b = jnp.where(low_lanes, b, half_roll(rows_of(part_b, base + j + 5)))
                out[d, 9 + j] = b.astype(BF16)


def add_kernel(ids, x, y, *outs):
    for n, out in enumerate(outs):
        d = 2 * (ids[2] ^ (n >> 1)) + (ids[1] ^ (n & 1))

        def step(j, carry):
            out[j] = (x[d, j].astype(F32) + y[d, j].astype(F32)).astype(BF16)
            return carry

        lax.fori_loop(0, 14, step, 0, unroll=2)


def middle_kernel(ids, x0, x1, x2, x3, vec, cache, out):
    low_lanes = lanes((48, 128)) < 64
    starts = ids[1] == 0
    bias, gain = vec[0:1], vec[1:2]

    def summed(tm, j):
        mine = x0[j].astype(F32) + x2[j].astype(F32)
        other = x1[j].astype(F32) + x3[j].astype(F32)
        return jnp.where(ids[1] == tm, mine, other)

    for j in range(5):
        b0, b1 = summed(0, 9 + j), summed(1, 9 + j)
        places = [(j, jnp.where(low_lanes, b0, half_roll(b1)))]
        if j < 4:
            places.append((j + 5, jnp.where(low_lanes, half_roll(b0), b1)))
        for c, b in places:
            hidden = jnp.concatenate([summed(0, c), summed(1, c), b], axis=1) + bias
            normed = norm_silu(hidden, gain).astype(BF16)
            out[c, 16:48] = normed[16:48]
            out[c, 0:16] = jnp.where(starts, cache[c], normed[0:16])


def second_kernel(ids, x, w, bias, out_own, out_peer, even, odd, low, high):
    def spread(c, carry):
        plane = x[c].astype(F32).reshape(6, 8, 384)
        for p in range(3):
            moved = shifted_rows(plane, p)
            even[p, c] = moved.reshape(48, 384).astype(BF16)
            odd[p, c] = moved[1:5].reshape(32, 384).astype(BF16)
        return carry

    lax.fori_loop(0, 18, spread, 0, unroll=2)

    def window(t):
        a, p, q = tap_of(t)
        if a == 1:
            rows = odd[p, q : q + 16]
        else:
            rows = even[p, q : q + 16, 8 * a : 8 * a + 32]
        return rows.reshape(512, 384)

    def kernel(t):
        a = [w[:, 3 * t + r].reshape(128, 128) for r in range(3)]
        b = [w[:, 81 + 3 * (t % 14) + r].reshape(128, 128) for r in range(3)]
        return jnp.concatenate([jnp.concatenate(a, axis=0), jnp.concatenate(b, axis=0)], axis=1)

    for begin, end, total in ((0, 14, low), (14, 27, high)):
        for t in range(begin, end, 2):
            taps = range(t, min(t + 2, end))
            left = jnp.concatenate([window(s) for s in taps], axis=1)
            right = jnp.concatenate([kernel(s) for s in taps], axis=0)
            product = jnp.dot(left, right, preferred_element_type=F32)
            if t == begin:
                total[...] = product
            else:
                total[...] += product

    first = ids[0] == 0
    bias = bias[...].reshape(1, 384)
    rest = bias[:, 256:]
    bias_a = jnp.where(first, bias[:, :128], bias[:, 128:256])
    bias_b = jnp.where(first, rest, half_roll(rest))
    low[:, :128] = low[:, :128] + high[:, :128] + bias_a
    low[:, 128:] = low[:, 128:] + half_roll(high[:, 128:]) + bias_b
    own = pl.multiple_of(256 * ids[0], 256)
    peer = pl.multiple_of(256 - 256 * ids[0], 256)
    out_own[...] = low[pl.ds(own, 256)]
    out_peer[...] = low[pl.ds(peer, 256)]


def last_kernel(ids, own, peer, video, out, rows):
    first = ids[0] == 0
    low_lanes = lanes((256, 128)) < 64
    rows[0] = jnp.where(first, own[:, :128], peer[:, :128])
    rows[1] = jnp.where(first, peer[:, :128], own[:, :128])
    b0 = jnp.where(first, own[:, 128:], peer[:, 128:])
    b1 = jnp.where(first, peer[:, 128:], own[:, 128:])
    rows[2] = jnp.where(low_lanes, b0, half_roll(b1))
    for f in range(4):
        for i in range(8):
            branch = every(rows, 8 * f + i, 32)
            out[f, i] = (video[f, i].astype(F32) + branch).astype(BF16)


def run(kernel, outs, scratch, args, scalars=1, flops=0, limit=48):
    specs = [pl.BlockSpec(memory_space=pltpu.SMEM)] * scalars
    specs += [pl.BlockSpec(memory_space=pltpu.VMEM)] * (len(args) - scalars)
    moved = sum(a.size * a.dtype.itemsize for a in args[scalars:])
    return pl.pallas_call(
        kernel,
        out_shape=outs,
        in_specs=specs,
        out_specs=jax.tree.map(lambda _: pl.BlockSpec(memory_space=pltpu.VMEM), outs),
        scratch_shapes=scratch,
        compiler_params=pltpu.CompilerParams(vmem_limit_bytes=limit * MIB),
        cost_estimate=pl.CostEstimate(flops=flops, bytes_accessed=moved, transcendentals=0),
    )(*args)


def shape(*dims, dtype=BF16):
    return jax.ShapeDtypeStruct(dims, dtype)


def per_device(video, gain1, w1, bias1, gain2, w2, bias2, cache1, cache2):
    ids = jnp.stack([lax.axis_index(a) for a in ("core", "tm", "xh", "y")]).astype(jnp.int32)

    sent1, sent2, edges = run(
        send_kernel,
        [shape(8, 124, 128), shape(16, 128, 128), shape(96, 384)],
        [pltpu.VMEM((128, 128), F32), pltpu.VMEM((3, 448, 128), F32), pltpu.VMEM((96, 384), F32)],
        [ids, w1.transpose(1, 0, 2), w2.transpose(1, 0, 2), video, cache1, cache2],
        limit=60,
    )
    near2 = lax.all_to_all(sent2, ("y", "xh", "core"), 0, 0)
    edges, near2 = lax.optimization_barrier((edges, near2))
    halo = lax.ppermute(edges, LON, [(i, (i + 1) % 128 if i % 2 else (i - 1) % 128) for i in range(128)])
    slices, cache_own, vectors = run(
        own_kernel,
        [shape(4, 320, 128), shape(8, 16, 384), shape(8, 384, dtype=F32)],
        [pltpu.VMEM((3, 448, 128), F32), pltpu.VMEM((320, 384), F32)],
        [ids, video, cache1, cache2, gain1, bias1, gain2],
    )
    entering, cache_rows = run(
        enter_kernel,
        [shape(8, 400, 128), shape(9, 16, 384)],
        [],
        [ids, slices, cache_own, vectors, halo],
    )
    turned2 = run(turn_kernel, shape(128, 16, 128), [pltpu.VMEM((2048, 128), F32)], [near2], scalars=0)
    kernel2 = lax.all_gather(turned2, "z", axis=0, tiled=False)
    sent1, near2 = lax.optimization_barrier((sent1, near2))
    near1 = lax.all_to_all(sent1, "z", 0, 0)
    kernel1 = [near1] + [lax.ppermute(near1, "y", [(i, (i + d) % 4) for i in range(4)]) for d in (1, 2, 3)]
    entering, near1 = lax.optimization_barrier((entering, near1))
    entered = lax.all_to_all(entering, RING, 0, 0)
    part_own, part_peer = run(
        first_kernel,
        [shape(4, 14, 48, 128), shape(4, 14, 48, 128)],
        [
            pltpu.VMEM((36, 10, 8, 128), F32),
            pltpu.VMEM((3, 36, 80, 128), BF16),
            pltpu.VMEM((3, 36, 64, 128), BF16),
            pltpu.VMEM((4096, 128), F32),
            pltpu.VMEM((27, 128, 256), BF16),
            pltpu.VMEM((34, 64, 128), F32),
            pltpu.VMEM((34, 64, 128), F32),
        ],
        [ids, entered, *kernel1],
        flops=2 * 2176 * 27 * 128 * 256,
    )
    part_peer = lax.ppermute(part_peer, "core", [(0, 1), (1, 0)])
    parts = run(add_kernel, [shape(14, 48, 128)] * 4, [], [ids, part_own, part_peer])
    summands = [parts[0]] + [
        lax.ppermute(parts[n], ("xh", "tm"), [(i, i ^ n) for i in range(4)]) for n in (1, 2, 3)
    ]
    second = run(middle_kernel, shape(9, 48, 384), [], [ids, *summands, vectors, cache_rows])
    pair = lax.all_gather(second, "core", axis=0, tiled=True)
    own, peer = run(
        second_kernel,
        [shape(256, 256, dtype=F32), shape(256, 256, dtype=F32)],
        [
            pltpu.VMEM((3, 18, 48, 384), BF16),
            pltpu.VMEM((3, 18, 32, 384), BF16),
            pltpu.VMEM((512, 256), F32),
            pltpu.VMEM((512, 256), F32),
        ],
        [ids, pair, kernel2, bias2],
        flops=2 * 512 * 27 * 384 * 256,
    )
    peer = lax.ppermute(peer, "core", [(0, 1), (1, 0)])
    return run(last_kernel, shape(4, 8, 8, 384), [pltpu.VMEM((3, 256, 128), F32)], [ids, own, peer, video])


def solution(mesh):
    ring = Mesh(mesh.devices.reshape(4, 8, 2, 2, 2), (*LON, "tm"))
    field = P("tm", None, LON, None)
    cache = P(None, None, LON, None)
    kernel = P(None, LON, None)
    return jax.shard_map(
        per_device,
        mesh=ring,
        in_specs=(field, P(), kernel, P(), P(), kernel, P(), cache, cache),
        out_specs=field,
        check_vma=False,
    )
```

time: 335 us -> 119 us (0.36)
  waiting for transfers between devices: 224 us -> 26.8 us
  local copies, waits for them, and re-layouts: 59 us -> 7.61 us
  blocking collectives: 0 us -> 22.9 us
  Pallas kernels: 0 us -> 20.9 us
  matrix products: 16.1 us -> 0 us
  starting transfers between devices: 11.4 us -> 26.4 us
  other arithmetic: 6.51 us -> 0.61 us
    all_gather x2 -> x1, waiting for transfers between devices: 211 us -> 0.01 us  [per_device(): kernel2 = lax.all_gather(turned2, 'z', axis=0, tiled=False)]
    slice x11 -> x0, local copies, waits for them, and re-layouts: 52.7 us -> none  [the longest x4 48.6 us: tap_terms(): kernel = piece[9 * frame_tap + 3 * row_tap + column_tap]]
    pallas_call x0 -> x9, Pallas kernels: none -> 20.9 us  [run(): pl.pallas_call(kernel, out_shape=outs, in_specs=specs, out_specs=jax.tree...]
    all_to_all x0 -> x1, blocking collectives: none -> 19.7 us  [per_device(): near2 = lax.all_to_all(sent2, ('y', 'xh', 'core'), 0, 0)]
    all_to_all x0 -> x2, starting transfers between devices: none -> 16.3 us  [the longest x1 8.2 us: per_device(): near1 = lax.all_to_all(sent1, 'z', 0, 0)]
    dot_general x54 -> x0, matrix products: 16.1 us -> none  [tap_terms(): jnp.dot(window.reshape(-1, width), kernel, preferred_element_type=jnp.flo...]
    ppermute x6 -> x9, waiting for transfers between devices: 12.4 us -> 25.7 us  [the longest x3 12.4 us: per_device(): lax.ppermute(near1, 'y', [(i, (i + d) % 4) for i in range(4)])]
    unnamed x78 -> x22, local copies, waits for them, and re-layouts: 6.2 us -> 7.61 us
  transfers between devices with their start and end apart: 8 -> 12, of which waited for: 7 -> 8; matrix products, arithmetic and copies ran while one was open for 20% -> 0% of each run, Pallas kernels for 0% -> 10%
where the time goes in v1:
time: 119 us
  waiting for transfers between devices  26.8 us (23%)
  starting transfers between devices  26.4 us (22%)
  blocking collectives  22.9 us (19%)
  Pallas kernels  20.9 us (18%)
  between operations  13.5 us (11%)
  local copies, waits for them, and re-layouts  7.61 us (6%)
    pallas_call x9, Pallas kernels, run(): pl.pallas_call(kernel, out_shape=outs, in_specs=specs, out_specs=jax.tree...  20.9 us
    all_to_all x1, blocking collectives, per_device(): near2 = lax.all_to_all(sent2, ('y', 'xh', 'core'), 0, 0)  19.7 us
    ppermute x3, waiting for transfers between devices, per_device(): lax.ppermute(near1, 'y', [(i, (i + d) % 4) for i in range(4)])  12.4 us
    ppermute x3, waiting for transfers between devices, per_device(): lax.ppermute(parts[n], ('xh', 'tm'), [(i, i ^ n) for i in range(4)])  10.3 us
    all_to_all x1, starting transfers between devices, per_device(): near1 = lax.all_to_all(sent1, 'z', 0, 0)  8.2 us
    all_to_all x1, starting transfers between devices, per_device(): entered = lax.all_to_all(entering, RING, 0, 0)  8.06 us
    unnamed x22, local copies, waits for them, and re-layouts  7.61 us
    ppermute x3, starting transfers between devices, per_device(): lax.ppermute(parts[n], ('xh', 'tm'), [(i, i ^ n) for i in range(4)])  3.95 us
  transfers between devices with their start and end apart: 12, of which 8 were waited for; matrix products, arithmetic and copies ran while one was open for 0% of the time, Pallas kernels for 10%

profile of v1, /device:TPU:1, one launch (start us, length us, event | category | flops | bytes accessed | tf_op | source)
XLA Modules:
  0.0 118.6 jit_solution(10873414741005775233)
XLA Ops:
  7.2 2.2 %shard_map.92 = (bf16[8,124,128]{2,1,0:T(8,128)(2,1)}, bf16[16,128,128]{2,1,0:T(8,128)(2,1)}, bf16[96,384]{1,0:T(8,128)(2,1)}) custom-call(s32[4]{0:T(128)} %pad_add_fusion.ids, bf16[3,27,384]{2,1,0:T(8,128)(2,1)} %bitcast.8, bf16[3,27,384]{2,1,0:T(8,128)(2,1)} %bitcast.9, bf16[4,8,8,384]{3,2,1,0:T(8,128)(2,1)} %video.5, bf16[2,8,8,384]{3,2,1,0:T(8,128)(2,1)} %cache1.3, ...), custom_call_target="tpu_custom_call" | custom-call | bytes 517632 | tf_op jit(solution)/shard_map/pallas_call | solution.py:356
  9.4 19.7 %all_to_all.15.x = bf16[16,128,128]{2,1,0:T(8,128)(2,1)S(1)} all-to-all(bf16[16,128,128]{2,1,0:T(8,128)(2,1)} %get-tuple-element.29), channel_id=1, replica_groups=mesh['y'=4,'z'=8,'xh'=2,'core'=2,'tm'=2] {'y','xh','core'}, dimensions={0} | all-to-all | bytes 1048576 | tf_op jit(solution)/shard_map/all_to_all | solution.py:381
  29.1 1.6 %shard_map.97 = bf16[128,16,128]{2,1,0:T(8,128)(2,1)} custom-call(bf16[16,128,128]{2,1,0:T(8,128)(2,1)S(1)} %all_to_all.15.x), custom_call_target="tpu_custom_call" | custom-call | bytes 524288 | tf_op jit(solution)/shard_map/pallas_call | solution.py:356
  30.7 8.2 %all-to-all-start.1 = ((bf16[8,124,128]{2,1,0:T(8,128)(2,1)}), bf16[8,124,128]{2,1,0:T(8,128)(2,1)S(1)}, u32[]{:S(2)}, u32[]{:S(2)}) async-start(bf16[8,124,128]{2,1,0:T(8,128)(2,1)} %get-tuple-element.34), calls=%async_computation.1 | async-start | bytes 524288 | tf_op jit(solution)/shard_map/all_to_all | solution.py:399
  38.9 1.9 %collective-permute-start = (bf16[96,384]{1,0:T(8,128)(2,1)}, bf16[96,384]{1,0:T(8,128)(2,1)S(1)}, u32[]{:S(2)}, u32[]{:S(2)}) collective-permute-start(bf16[96,384]{1,0:T(8,128)(2,1)} %get-tuple-element.30), channel_id=1, source_target_pairs={{0,254},{2,4},{4,2},{6,8},{8,6},{10,12},{12,10},{14,16},{16,14},{1... | collective-permute-start | bytes 221192 | tf_op jit(solution)/shard_map/ppermute | solution.py:383
  46.2 1.5 %shard_map.91 = (bf16[4,320,128]{2,1,0:T(8,128)(2,1)S(1)}, bf16[8,16,384]{2,1,0:T(8,128)(2,1)S(1)}, f32[8,384]{1,0:T(8,128)S(1)}) custom-call(s32[4]{0:T(128)S(1)} %copy-done.4, bf16[4,8,8,384]{3,2,1,0:T(8,128)(2,1)S(1)} %copy-done, bf16[2,8,8,384]{3,2,1,0:T(8,128)(2,1)S(1)} %copy-done.2, bf16[2,8,8,384]{3,2,1,0:T(8,128)(2,1)S(1)} %copy-done.3, ...), custom_call_target="tpu_custom_call" | custom-call | bytes 397824 | tf_op jit(solution)/shard_map/pallas_call | solution.py:356
  47.7 1.9 %shard_map.93 = (bf16[8,400,128]{2,1,0:T(8,128)(2,1)}, bf16[9,16,384]{2,1,0:T(8,128)(2,1)S(1)}) custom-call(s32[4]{0:T(128)S(1)} %copy-done.4, bf16[4,320,128]{2,1,0:T(8,128)(2,1)S(1)} %get-tuple-element.25.own, bf16[8,16,384]{2,1,0:T(8,128)(2,1)S(1)} %get-tuple-element.26.cache, f32[8,384]{1,0:T(8,128)S(1)} %get-tuple-element.27.vec, ...), custom_call_target="tpu_custom_call" | custom-call | bytes 512000 | tf_op jit(solution)/shard_map/pallas_call | solution.py:356
  49.6 1.1 all-to-all-done.1.w0
  50.7 8.1 %all-to-all-start.2 = ((bf16[8,400,128]{2,1,0:T(8,128)(2,1)}), bf16[8,400,128]{2,1,0:T(8,128)(2,1)S(1)}, u32[]{:S(2)}, u32[]{:S(2)}) async-start(bf16[8,400,128]{2,1,0:T(8,128)(2,1)} %get-tuple-element.35), calls=%async_computation.2 | async-start | bytes 1638400 | tf_op jit(solution)/shard_map/all_to_all | solution.py:402
  59.5 1.9 %collective-permute-start.3 = (bf16[8,124,128]{2,1,0:T(8,128)(2,1)S(1)}, bf16[8,124,128]{2,1,0:T(8,128)(2,1)S(1)}, u32[]{:S(2)}, u32[]{:S(2)}) collective-permute-start(bf16[8,124,128]{2,1,0:T(8,128)(2,1)S(1)} %all-to-all-done.1.w0), channel_id=1, source_target_pairs={{0,192},{64,0},{128,64},{192,128},{1,193},{65,1},{129,65},{193,129... | collective-permute-start | bytes 761864 | tf_op jit(solution)/shard_map/ppermute | solution.py:400
  61.5 12.1 %collective-permute-done.1.w1 = bf16[8,124,128]{2,1,0:T(8,128)(2,1)S(1)} collective-permute-done((bf16[8,124,128]{2,1,0:T(8,128)(2,1)S(1)}, bf16[8,124,128]{2,1,0:T(8,128)(2,1)S(1)}, u32[]{:S(2)}, u32[]{:S(2)}) %collective-permute-start.1) | collective-permute-done | bytes 253984 | tf_op jit(solution)/shard_map/ppermute | solution.py:400
  73.9 6.2 %shard_map.94 = (bf16[4,14,48,128]{3,2,1,0:T(8,128)(2,1)S(1)}, bf16[4,14,48,128]{3,2,1,0:T(8,128)(2,1)S(1)}) custom-call(s32[4]{0:T(128)S(1)} %copy-done.5, bf16[8,400,128]{2,1,0:T(8,128)(2,1)S(1)} %all-to-all-done.2.x, bf16[8,124,128]{2,1,0:T(8,128)(2,1)S(1)} %all-to-all-done.1.w0, bf16[8,124,128]{2,1,0:T(8,128)(2,1)S(1)} %collective-permute-done.1.w1, ...), custom_call_target="tpu_custom_call" | custom-call | flops 3850371072 | bytes 1835008 | tf_op jit(solution)/shard_map/pallas_call | solution.py:356
  80.1 1.2 collective-permute-start.4
  81.3 1.8 %collective-permute-done.4.y = bf16[4,14,48,128]{3,2,1,0:T(8,128)(2,1)S(1)} collective-permute-done((bf16[4,14,48,128]{3,2,1,0:T(8,128)(2,1)S(1)}, bf16[4,14,48,128]{3,2,1,0:T(8,128)(2,1)S(1)}, u32[]{:S(2)}, u32[]{:S(2)}) %collective-permute-start.4) | collective-permute-done | bytes 688160 | tf_op jit(solution)/shard_map/ppermute | solution.py:418
  83.9 1.5 %collective-permute-start.5 = (bf16[14,48,128]{2,1,0:T(8,128)(2,1)S(1)}, bf16[14,48,128]{2,1,0:T(8,128)(2,1)S(1)}, u32[]{:S(2)}, u32[]{:S(2)}) collective-permute-start(bf16[14,48,128]{2,1,0:T(8,128)(2,1)S(1)} %get-tuple-element.39), channel_id=1, source_target_pairs={{0,1},{1,0},{4,5},{5,4},{2,3},{3,2},{6,7},{7,6},{8,9},{9,8},{12,13... | collective-permute-start | bytes 516104 | tf_op jit(solution)/shard_map/ppermute | solution.py:421
  85.4 2.4 %collective-permute-start.6 = (bf16[14,48,128]{2,1,0:T(8,128)(2,1)S(1)}, bf16[14,48,128]{2,1,0:T(8,128)(2,1)S(1)}, u32[]{:S(2)}, u32[]{:S(2)}) collective-permute-start(bf16[14,48,128]{2,1,0:T(8,128)(2,1)S(1)} %get-tuple-element.40), channel_id=1, source_target_pairs={{0,4},{1,5},{4,0},{5,1},{2,6},{3,7},{6,2},{7,3},{8,12},{9,13},{12,... | collective-permute-start | bytes 516104 | tf_op jit(solution)/shard_map/ppermute | solution.py:421
  87.9 1.7 %collective-permute-done.5.x1 = bf16[14,48,128]{2,1,0:T(8,128)(2,1)S(1)} collective-permute-done((bf16[14,48,128]{2,1,0:T(8,128)(2,1)S(1)}, bf16[14,48,128]{2,1,0:T(8,128)(2,1)S(1)}, u32[]{:S(2)}, u32[]{:S(2)}) %collective-permute-start.5) | collective-permute-done | bytes 172064 | tf_op jit(solution)/shard_map/ppermute | solution.py:421
  89.6 6.0 %collective-permute-done.6.x2 = bf16[14,48,128]{2,1,0:T(8,128)(2,1)S(1)} collective-permute-done((bf16[14,48,128]{2,1,0:T(8,128)(2,1)S(1)}, bf16[14,48,128]{2,1,0:T(8,128)(2,1)S(1)}, u32[]{:S(2)}, u32[]{:S(2)}) %collective-permute-start.6) | collective-permute-done | bytes 172064 | tf_op jit(solution)/shard_map/ppermute | solution.py:421
  95.6 2.6 %collective-permute-done.7.x3 = bf16[14,48,128]{2,1,0:T(8,128)(2,1)S(1)} collective-permute-done((bf16[14,48,128]{2,1,0:T(8,128)(2,1)S(1)}, bf16[14,48,128]{2,1,0:T(8,128)(2,1)S(1)}, u32[]{:S(2)}, u32[]{:S(2)}) %collective-permute-start.7) | collective-permute-done | bytes 172064 | tf_op jit(solution)/shard_map/ppermute | solution.py:421
  99.2 3.2 %all_gather.9.x = bf16[18,48,384]{2,1,0:T(8,128)(2,1)S(1)} all-gather(bf16[9,48,384]{2,1,0:T(8,128)(2,1)S(1)} %shard_map.96), channel_id=1, replica_groups=mesh['y'=4,'z'=8,'xh'=2,'core'=2,'tm'=2] {'core'}, dimensions={0}, use_global_device_ids=true | all-gather | bytes 995328 | tf_op jit(solution)/shard_map/all_gather | solution.py:424
  102.4 2.2 %copy-done.9 = bf16[1024,16,128]{2,1,0:T(8,128)(2,1)S(1)} copy-done((bf16[1024,16,128]{2,1,0:T(8,128)(2,1)S(1)}, bf16[1024,16,128]{2,1,0:T(8,128)(2,1)}, u32[]{:S(2)}) %copy-start.9) | copy-done | bytes 4194328
  104.6 4.0 %shard_map.98 = (f32[256,256]{1,0:T(8,128)S(1)}, f32[256,256]{1,0:T(8,128)S(1)}) custom-call(s32[4]{0:T(128)S(1)} %copy-done.5, bf16[18,48,384]{2,1,0:T(8,128)(2,1)S(1)} %all_gather.9.x, bf16[8,128,16,128]{3,2,1,0:T(8,128)(2,1)S(1)} %bitcast.7, f32[384]{0:T(512)S(1)} %copy-done.10), custom_call_target="tpu_custom_call" | custom-call | flops 2717908992 | bytes 4859392 | tf_op jit(solution)/shard_map/pallas_call | solution.py:356
  109.0 1.2 collective-permute-done.8.peer
  110.2 1.6 %shard_map.99 = bf16[4,8,8,384]{3,2,1,0:T(8,128)(2,1)} custom-call(s32[4]{0:T(128)S(1)} %copy-done.5, f32[256,256]{1,0:T(8,128)S(1)} %get-tuple-element.43.own, f32[256,256]{1,0:T(8,128)S(1)} %collective-permute-done.8.peer, bf16[4,8,8,384]{3,2,1,0:T(8,128)(2,1)S(1)} %copy-done.1), custom_call_target="tpu_custom_call" | custom-call | bytes 720896 | tf_op jit(solution)/shard_map/pallas_call | solution.py:356
  (35 shorter events, 9.6 us)
Async XLA Ops:
  6.5 95.9 %all-gather.3.cloned.1.call-start = ((), (), s32[]{:S(2)}) async-start(), calls=%async_computation.3 | async-start | bytes 4718592 | tf_op jit(solution)/shard_map/all_gather | solution.py:397
  7.2 66.7 %copy-start.5 = (s32[4]{0:T(128)S(1)}, s32[4]{0:T(128)}, u32[]{:S(2)}) copy-start(s32[4]{0:T(128)} %pad_add_fusion.ids) | copy-start | bytes 52
  30.7 20.0 %all-to-all-start.1 = ((bf16[8,124,128]{2,1,0:T(8,128)(2,1)}), bf16[8,124,128]{2,1,0:T(8,128)(2,1)S(1)}, u32[]{:S(2)}, u32[]{:S(2)}) async-start(bf16[8,124,128]{2,1,0:T(8,128)(2,1)} %get-tuple-element.34), calls=%async_computation.1 | async-start | bytes 524288 | tf_op jit(solution)/shard_map/all_to_all | solution.py:399
  38.9 8.8 %collective-permute-start = (bf16[96,384]{1,0:T(8,128)(2,1)}, bf16[96,384]{1,0:T(8,128)(2,1)S(1)}, u32[]{:S(2)}, u32[]{:S(2)}) collective-permute-start(bf16[96,384]{1,0:T(8,128)(2,1)} %get-tuple-element.30), channel_id=1, source_target_pairs={{0,254},{2,4},{4,2},{6,8},{8,6},{10,12},{12,10},{14,16},{16,14},{1... | collective-permute-start | bytes 221192 | tf_op jit(solution)/shard_map/ppermute | solution.py:383
  40.8 1.0 copy-start
  41.7 0.9 copy-start.2
  42.6 0.9 copy-start.3
  43.5 0.6 copy-start.4
  44.2 0.7 copy-start.6
  44.8 0.7 copy-start.7
  45.5 0.7 copy-start.8
  50.7 23.2 %all-to-all-start.2 = ((bf16[8,400,128]{2,1,0:T(8,128)(2,1)}), bf16[8,400,128]{2,1,0:T(8,128)(2,1)S(1)}, u32[]{:S(2)}, u32[]{:S(2)}) async-start(bf16[8,400,128]{2,1,0:T(8,128)(2,1)} %get-tuple-element.35), calls=%async_computation.2 | async-start | bytes 1638400 | tf_op jit(solution)/shard_map/all_to_all | solution.py:402
  58.8 43.6 %copy-start.10 = (f32[384]{0:T(512)S(1)}, f32[384]{0:T(512)}, u32[]{:S(2)}) copy-start(f32[384]{0:T(512)} %bias.1) | copy-start | bytes 4612
  58.8 14.8 %collective-permute-start.1 = (bf16[8,124,128]{2,1,0:T(8,128)(2,1)S(1)}, bf16[8,124,128]{2,1,0:T(8,128)(2,1)S(1)}, u32[]{:S(2)}, u32[]{:S(2)}) collective-permute-start(bf16[8,124,128]{2,1,0:T(8,128)(2,1)S(1)} %all-to-all-done.1.w0), channel_id=1, source_target_pairs={{0,64},{64,128},{128,192},{192,0},{1,65},{65,129},{129,193},{193,1... | collective-permute-start | bytes 761864 | tf_op jit(solution)/shard_map/ppermute | solution.py:400
  58.8 14.8 %collective-permute-start.2 = (bf16[8,124,128]{2,1,0:T(8,128)(2,1)S(1)}, bf16[8,124,128]{2,1,0:T(8,128)(2,1)S(1)}, u32[]{:S(2)}, u32[]{:S(2)}) collective-permute-start(bf16[8,124,128]{2,1,0:T(8,128)(2,1)S(1)} %all-to-all-done.1.w0), channel_id=1, source_target_pairs={{0,128},{64,192},{128,0},{192,64},{1,129},{65,193},{129,1},{193,65... | collective-permute-start | bytes 761864 | tf_op jit(solution)/shard_map/ppermute | solution.py:400
  59.5 14.4 %collective-permute-start.3 = (bf16[8,124,128]{2,1,0:T(8,128)(2,1)S(1)}, bf16[8,124,128]{2,1,0:T(8,128)(2,1)S(1)}, u32[]{:S(2)}, u32[]{:S(2)}) collective-permute-start(bf16[8,124,128]{2,1,0:T(8,128)(2,1)S(1)} %all-to-all-done.1.w0), channel_id=1, source_target_pairs={{0,192},{64,0},{128,64},{192,128},{1,193},{65,1},{129,65},{193,129... | collective-permute-start | bytes 761864 | tf_op jit(solution)/shard_map/ppermute | solution.py:400
  80.1 2.9 %collective-permute-start.4 = (bf16[4,14,48,128]{3,2,1,0:T(8,128)(2,1)S(1)}, bf16[4,14,48,128]{3,2,1,0:T(8,128)(2,1)S(1)}, u32[]{:S(2)}, u32[]{:S(2)}) collective-permute-start(bf16[4,14,48,128]{3,2,1,0:T(8,128)(2,1)S(1)} %get-tuple-element.37), channel_id=1, source_target_pairs={{0,2},{2,0},{1,3},{3,1},{4,6},{6,4},{5,7},{7,5},{8,10},{10,8},{9,1... | collective-permute-start | bytes 2064392 | tf_op jit(solution)/shard_map/ppermute | solution.py:418
  83.9 5.7 %collective-permute-start.5 = (bf16[14,48,128]{2,1,0:T(8,128)(2,1)S(1)}, bf16[14,48,128]{2,1,0:T(8,128)(2,1)S(1)}, u32[]{:S(2)}, u32[]{:S(2)}) collective-permute-start(bf16[14,48,128]{2,1,0:T(8,128)(2,1)S(1)} %get-tuple-element.39), channel_id=1, source_target_pairs={{0,1},{1,0},{4,5},{5,4},{2,3},{3,2},{6,7},{7,6},{8,9},{9,8},{12,13... | collective-permute-start | bytes 516104 | tf_op jit(solution)/shard_map/ppermute | solution.py:421
  85.4 10.2 %collective-permute-start.6 = (bf16[14,48,128]{2,1,0:T(8,128)(2,1)S(1)}, bf16[14,48,128]{2,1,0:T(8,128)(2,1)S(1)}, u32[]{:S(2)}, u32[]{:S(2)}) collective-permute-start(bf16[14,48,128]{2,1,0:T(8,128)(2,1)S(1)} %get-tuple-element.40), channel_id=1, source_target_pairs={{0,4},{1,5},{4,0},{5,1},{2,6},{3,7},{6,2},{7,3},{8,12},{9,13},{12,... | collective-permute-start | bytes 516104 | tf_op jit(solution)/shard_map/ppermute | solution.py:421
  87.8 10.4 %collective-permute-start.7 = (bf16[14,48,128]{2,1,0:T(8,128)(2,1)S(1)}, bf16[14,48,128]{2,1,0:T(8,128)(2,1)S(1)}, u32[]{:S(2)}, u32[]{:S(2)}) collective-permute-start(bf16[14,48,128]{2,1,0:T(8,128)(2,1)S(1)} %get-tuple-element.41), channel_id=1, source_target_pairs={{0,5},{1,4},{4,1},{5,0},{2,7},{3,6},{6,3},{7,2},{8,13},{9,12},{12,... | collective-permute-start | bytes 516104 | tf_op jit(solution)/shard_map/ppermute | solution.py:421
  102.4 2.2 %copy-start.9 = (bf16[1024,16,128]{2,1,0:T(8,128)(2,1)S(1)}, bf16[1024,16,128]{2,1,0:T(8,128)(2,1)}, u32[]{:S(2)}) copy-start(bf16[1024,16,128]{2,1,0:T(8,128)(2,1)} %all-gather.3.cloned.1.call-done) | copy-start | bytes 12582916
  104.6 5.6 %copy-start.1 = (bf16[4,8,8,384]{3,2,1,0:T(8,128)(2,1)S(1)}, bf16[4,8,8,384]{3,2,1,0:T(8,128)(2,1)}, u32[]{:S(2)}) copy-start(bf16[4,8,8,384]{3,2,1,0:T(8,128)(2,1)} %video.5) | copy-start | bytes 589828
  108.6 1.6 %collective-permute-start.8 = (f32[256,256]{1,0:T(8,128)S(1)}, f32[256,256]{1,0:T(8,128)S(1)}, u32[]{:S(2)}, u32[]{:S(2)}) collective-permute-start(f32[256,256]{1,0:T(8,128)S(1)} %get-tuple-element.44), channel_id=1, source_target_pairs={{0,2},{2,0},{1,3},{3,1},{4,6},{6,4},{5,7},{7,5},{8,10},{10,8},{9,1... | collective-permute-start | bytes 786440 | tf_op jit(solution)/shard_map/ppermute | solution.py:437
Sparse Core Ops, SparseCore 0:
  30.9 57.6 all-gather.2

commit v2 on v1

--- a/solution.py
+++ b/solution.py
@@ -1,3 +1,5 @@
+import functools
+
 import jax
 import jax.numpy as jnp
 from jax import lax
@@ -9,9 +11,14 @@
 LON = ("y", "z", "xh", "core")
 RING = ("xh", "core", "tm")
 PLANE = ("y", "z")
+SWAP = [(0, 1), (1, 0)]
 F32 = jnp.float32
 BF16 = jnp.bfloat16
 MIB = 1 << 20
+
+
+def position():
+    return [lax.axis_index(a) for a in ("core", "tm", "xh", "y")]
 
 
 def lanes(shape):
@@ -64,20 +71,22 @@
     slot[123:] = jnp.zeros((5, 128), F32)
 
 
-def send_kernel(ids, w1, w2, video, cache1, cache2, out1, out2, out_edge, slot, wide, edge):
-    taps2 = [w2[r].astype(F32) for r in range(3)]
-    for half in range(2):
-        pack(slot, taps2, half)
-        packed = slot[...].astype(BF16)
-        for n in range(8):
-            out2[2 * n + half] = packed
-    order = order_matrix().astype(BF16)
-    taps1 = [jnp.dot(w1[r], order, preferred_element_type=F32) for r in range(3)]
-    pack(slot, taps1, ids[1])
-    packed = slot[:124].astype(BF16)
-    for n in range(8):
-        out1[n] = packed
-
+def by_slice(x, gain):
+    frame = lax.rem(lax.broadcasted_iota(jnp.int32, x.shape, 0) >> 3, 5)
+    x = jnp.where(frame == 4, x, norm_silu(x, gain)).astype(BF16)
+    return jnp.dot(x, spread_matrix().astype(BF16), preferred_element_type=F32).astype(BF16)
+
+
+def ordered(x):
+    return jnp.dot(x.astype(BF16), order_matrix().astype(BF16), preferred_element_type=F32).astype(BF16)
+
+
+def pack_kernel(w2, video, cache1, cache2, mine, peer, out_edge, slot, wide, edge):
+    ids = position()
+    taps = [w2[r].astype(F32) for r in range(3)]
+    for half, out in ((ids[0], mine), (1 - ids[0], peer)):
+        pack(slot, taps, half)
+        out[...] = slot[:124].astype(BF16)
     upper = ids[0] == 1
     put(wide, 0, video[...].astype(F32).reshape(256, 384))
     put(wide, 256, cache1[ids[1]].astype(F32).reshape(64, 384))
@@ -95,27 +104,19 @@
     out_edge[...] = edge[...].astype(BF16)
 
 
-def turn_kernel(x, out, wide):
-    wide[...] = x[...].astype(F32).reshape(2048, 128)
-
-    def step(row, carry):
-        out[row] = wide[pl.ds(row, 16, stride=128), :].astype(BF16)
-        return carry
-
-    lax.fori_loop(0, 128, step, 0, unroll=8)
-
-
-def by_slice(x, gain):
-    frame = lax.rem(lax.broadcasted_iota(jnp.int32, x.shape, 0) >> 3, 5)
-    x = jnp.where(frame == 4, x, norm_silu(x, gain)).astype(BF16)
-    return jnp.dot(x, spread_matrix().astype(BF16), preferred_element_type=F32).astype(BF16)
-
-
-def ordered(x):
-    return jnp.dot(x.astype(BF16), order_matrix().astype(BF16), preferred_element_type=F32).astype(BF16)
-
-
-def own_kernel(ids, video, cache1, cache2, gain1, bias1, gain2, out, out_cache, out_vec, wide, rows):
+def send_kernel(
+    w1, video, cache1, cache2, gain1, bias1, gain2,
+    out1, out, out_cache, out_vec,
+    slot, wide, rows,
+):
+    ids = position()
+    order = order_matrix().astype(BF16)
+    taps1 = [jnp.dot(w1[r], order, preferred_element_type=F32) for r in range(3)]
+    pack(slot, taps1, ids[1])
+    packed = slot[:124].astype(BF16)
+    for n in range(8):
+        out1[n] = packed
+
     put(wide, 0, video[...].astype(F32).reshape(256, 384))
     put(wide, 256, cache1[ids[1]].astype(F32).reshape(64, 384))
     put(wide, 320, cache2[...].astype(F32).reshape(128, 384))
@@ -139,12 +140,35 @@
     out_vec[...] = jnp.concatenate([placed[:2], vectors[2:]], axis=0)
 
 
-def enter_kernel(ids, own, cache, vec, halo, out, out_cache):
+def join_kernel(axis, mine, other, out):
+    at = position()[axis]
+    out[at] = mine[...]
+    out[1 - at] = other[...]
+
+
+def turn_kernel(w0, w1, w2, w3, out, wide):
+    y = position()[3]
+    for d, w in enumerate((w0, w1, w2, w3)):
+        at = pl.multiple_of(512 * ((y + 4 - d) & 3), 512)
+        for n in range(4):
+            wide[pl.ds(at + 128 * n, 124), :] = w[n].astype(F32)
+
+    def step(row, carry):
+        out[row] = wide[pl.ds(row, 16, stride=128), :].astype(BF16)
+        return carry
+
+    lax.fori_loop(0, 124, step, 0, unroll=4)
+
+
+def enter_kernel(own, cache, vec, halo, keep, give, out_cache, edge):
+    ids = position()
     slices = by_slice(halo[0:80].astype(F32), vec[2:3])
     for q in range(4):
-        for tm in range(2):
-            out[2 * q + tm, 0:320] = own[q]
-            out[2 * q + tm, 320:400] = slices[:, 128 * q : 128 * q + 128]
+        edge[q] = slices[:, 128 * q : 128 * q + 128]
+    for xh in range(2):
+        for out, core in ((keep, ids[0]), (give, 1 - ids[0])):
+            out[xh, 0:320] = own[2 * xh + core]
+            out[xh, 320:400] = edge[2 * xh + core]
     beyond = ordered(halo[80:96])
 
     @pl.when(ids[0] == 0)
@@ -156,6 +180,14 @@
     def _():
         out_cache[0:8] = cache[...]
         out_cache[8] = beyond
+
+
+def arrange_kernel(keep, got, same, across):
+    ids = position()
+    same[0] = keep[ids[2]]
+    same[1] = got[ids[2]]
+    across[0] = keep[1 - ids[2]]
+    across[1] = got[1 - ids[2]]
 
 
 def shifted_rows(x, p):
@@ -172,19 +204,21 @@
     return t // 9, (t // 3) % 3, t % 3
 
 
-def first_kernel(ids, x, w0, w1, w2, w3, out_own, out_peer, field, even, odd, wide, kernel, part_a, part_b):
-    for s in range(8):
-        q, tm = s // 2, s % 2
-        piece = x[s].astype(F32).reshape(10, 5, 8, 128)
-        places = [(2 + 8 * q, 0, 8)]
-        if q == 0:
-            places.append((0, 8, 10))
-        if q == 3:
-            places.append((34, 8, 10))
-        for at, begin, end in places:
-            n = end - begin
-            field[at : at + n, 2 + 4 * tm : 6 + 4 * tm] = piece[begin:end, 0:4]
-            field[at : at + n, tm] = piece[begin:end, 4]
+def first_kernel(x0, x1, x2, x3, w0, w1, w2, w3, out_own, out_peer, field, even, odd, wide, kernel, part_a, part_b):
+    ids = position()
+    for n, x in enumerate((x0, x1, x2, x3)):
+        tm = ids[1] ^ (n & 1)
+        for m in range(2):
+            q = 2 * (ids[2] ^ (n >> 1)) + (ids[0] ^ m)
+            piece = x[m].astype(F32).reshape(10, 5, 8, 128)
+
+            def place(at, begin, end):
+                field[pl.ds(at, end - begin), pl.ds(2 + 4 * tm, 4)] = piece[begin:end, 0:4]
+                field[pl.ds(at, end - begin), tm] = piece[begin:end, 4]
+
+            place(2 + 8 * q, 0, 8)
+            pl.when(q == 0)(lambda: place(0, 8, 10))
+            pl.when(q == 3)(lambda: place(34, 8, 10))
 
     def spread(c, carry):
         plane = field[c]
@@ -254,7 +288,8 @@
                 out[d, 9 + j] = b.astype(BF16)
 
 
-def add_kernel(ids, x, y, *outs):
+def add_kernel(x, y, *outs):
+    ids = position()
     for n, out in enumerate(outs):
         d = 2 * (ids[2] ^ (n >> 1)) + (ids[1] ^ (n & 1))
 
@@ -265,7 +300,8 @@
         lax.fori_loop(0, 14, step, 0, unroll=2)
 
 
-def middle_kernel(ids, x0, x1, x2, x3, vec, cache, out):
+def middle_kernel(x0, x1, x2, x3, vec, cache, out):
+    ids = position()
     low_lanes = lanes((48, 128)) < 64
     starts = ids[1] == 0
     bias, gain = vec[0:1], vec[1:2]
@@ -287,16 +323,19 @@
             out[c, 0:16] = jnp.where(starts, cache[c], normed[0:16])
 
 
-def second_kernel(ids, x, w, bias, out_own, out_peer, even, odd, low, high):
+def second_kernel(mine, other, w, bias, out_own, out_peer, even, odd, low, high):
+    ids = position()
     def spread(c, carry):
-        plane = x[c].astype(F32).reshape(6, 8, 384)
-        for p in range(3):
-            moved = shifted_rows(plane, p)
-            even[p, c] = moved.reshape(48, 384).astype(BF16)
-            odd[p, c] = moved[1:5].reshape(32, 384).astype(BF16)
+        for x, core in ((mine, ids[0]), (other, 1 - ids[0])):
+            plane = x[c].astype(F32).reshape(6, 8, 384)
+            at = 9 * core + c
+            for p in range(3):
+                moved = shifted_rows(plane, p)
+                even[p, at] = moved.reshape(48, 384).astype(BF16)
+                odd[p, at] = moved[1:5].reshape(32, 384).astype(BF16)
         return carry
 
-    lax.fori_loop(0, 18, spread, 0, unroll=2)
+    lax.fori_loop(0, 9, spread, 0)
 
     def window(t):
         a, p, q = tap_of(t)
@@ -335,7 +374,8 @@
     out_peer[...] = low[pl.ds(peer, 256)]
 
 
-def last_kernel(ids, own, peer, video, out, rows):
+def last_kernel(own, peer, video, out, rows):
+    ids = position()
     first = ids[0] == 0
     low_lanes = lanes((256, 128)) < 64
     rows[0] = jnp.where(first, own[:, :128], peer[:, :128])
@@ -349,10 +389,9 @@
             out[f, i] = (video[f, i].astype(F32) + branch).astype(BF16)
 
 
-def run(kernel, outs, scratch, args, scalars=1, flops=0, limit=48):
-    specs = [pl.BlockSpec(memory_space=pltpu.SMEM)] * scalars
-    specs += [pl.BlockSpec(memory_space=pltpu.VMEM)] * (len(args) - scalars)
-    moved = sum(a.size * a.dtype.itemsize for a in args[scalars:])
+def run(kernel, outs, scratch, args, flops=0, limit=48):
+    specs = [pl.BlockSpec(memory_space=pltpu.VMEM)] * len(args)
+    moved = sum(a.size * a.dtype.itemsize for a in args)
     return pl.pallas_call(
         kernel,
         out_shape=outs,
@@ -364,42 +403,64 @@
     )(*args)
 
 
+def round_y(x):
+    return [lax.ppermute(x, "y", [(i, (i + d) % 4) for i in range(4)]) for d in (1, 2, 3)]
+
+
 def shape(*dims, dtype=BF16):
     return jax.ShapeDtypeStruct(dims, dtype)
 
 
 def per_device(video, gain1, w1, bias1, gain2, w2, bias2, cache1, cache2):
-    ids = jnp.stack([lax.axis_index(a) for a in ("core", "tm", "xh", "y")]).astype(jnp.int32)
-
-    sent1, sent2, edges = run(
+    w1, w2 = w1.transpose(1, 0, 2), w2.transpose(1, 0, 2)
+    mine2, peer2, edges = run(
+        pack_kernel,
+        [shape(124, 128), shape(124, 128), shape(96, 384)],
+        [pltpu.VMEM((128, 128), F32), pltpu.VMEM((3, 448, 128), F32), pltpu.VMEM((96, 384), F32)],
+        [w2, video, cache1, cache2],
+        limit=60,
+    )
+    peer2 = lax.ppermute(peer2, "core", SWAP)
+    pair2 = run(functools.partial(join_kernel, 0), shape(2, 124, 128), [], [mine2, peer2])
+    pair2, w1 = lax.optimization_barrier((pair2, w1))
+    sent1, slices, cache_own, vectors = run(
         send_kernel,
-        [shape(8, 124, 128), shape(16, 128, 128), shape(96, 384)],
-        [pltpu.VMEM((128, 128), F32), pltpu.VMEM((3, 448, 128), F32), pltpu.VMEM((96, 384), F32)],
-        [ids, w1.transpose(1, 0, 2), w2.transpose(1, 0, 2), video, cache1, cache2],
+        [
+            shape(8, 124, 128),
+            shape(4, 320, 128),
+            shape(8, 16, 384),
+            shape(8, 384, dtype=F32),
+        ],
+        [
+            pltpu.VMEM((128, 128), F32),
+            pltpu.VMEM((3, 448, 128), F32),
+            pltpu.VMEM((320, 384), F32),
+        ],
+        [w1, video, cache1, cache2, gain1, bias1, gain2],
         limit=60,
     )
-    near2 = lax.all_to_all(sent2, ("y", "xh", "core"), 0, 0)
-    edges, near2 = lax.optimization_barrier((edges, near2))
+    other2 = lax.ppermute(pair2, "xh", SWAP)
+    quad2 = run(functools.partial(join_kernel, 2), shape(2, 2, 124, 128), [], [pair2, other2])
+    quad2 = quad2.reshape(4, 124, 128)
+    quad2, sent1 = lax.optimization_barrier((quad2, sent1))
+    near2 = [quad2, *round_y(quad2)]
     halo = lax.ppermute(edges, LON, [(i, (i + 1) % 128 if i % 2 else (i - 1) % 128) for i in range(128)])
-    slices, cache_own, vectors = run(
-        own_kernel,
-        [shape(4, 320, 128), shape(8, 16, 384), shape(8, 384, dtype=F32)],
-        [pltpu.VMEM((3, 448, 128), F32), pltpu.VMEM((320, 384), F32)],
-        [ids, video, cache1, cache2, gain1, bias1, gain2],
-    )
-    entering, cache_rows = run(
+    turned2 = run(turn_kernel, shape(124, 16, 128), [pltpu.VMEM((2048, 128), F32)], near2)
+    sent1, turned2, halo = lax.optimization_barrier((sent1, turned2, halo))
+    near1 = lax.all_to_all(sent1, "z", 0, 0)
+    kernel2 = lax.all_gather(turned2, "z", axis=0, tiled=False)
+    keep, give, cache_rows = run(
         enter_kernel,
-        [shape(8, 400, 128), shape(9, 16, 384)],
-        [],
-        [ids, slices, cache_own, vectors, halo],
-    )
-    turned2 = run(turn_kernel, shape(128, 16, 128), [pltpu.VMEM((2048, 128), F32)], [near2], scalars=0)
-    kernel2 = lax.all_gather(turned2, "z", axis=0, tiled=False)
-    sent1, near2 = lax.optimization_barrier((sent1, near2))
-    near1 = lax.all_to_all(sent1, "z", 0, 0)
-    kernel1 = [near1] + [lax.ppermute(near1, "y", [(i, (i + d) % 4) for i in range(4)]) for d in (1, 2, 3)]
-    entering, near1 = lax.optimization_barrier((entering, near1))
-    entered = lax.all_to_all(entering, RING, 0, 0)
+        [shape(2, 400, 128), shape(2, 400, 128), shape(9, 16, 384)],
+        [pltpu.VMEM((4, 80, 128), BF16)],
+        [slices, cache_own, vectors, halo],
+    )
+    got = lax.ppermute(give, "core", SWAP)
+    same, across = run(arrange_kernel, [shape(2, 400, 128)] * 2, [], [keep, got])
+    entered = [same] + [
+        lax.ppermute(v, ("xh", "tm"), [(i, i ^ n) for i in range(4)]) for n, v in ((1, same), (2, across), (3, across))
+    ]
+    kernel1 = [near1, *round_y(near1)]
     part_own, part_peer = run(
         first_kernel,
         [shape(4, 14, 48, 128), shape(4, 14, 48, 128)],
@@ -412,16 +473,17 @@
             pltpu.VMEM((34, 64, 128), F32),
             pltpu.VMEM((34, 64, 128), F32),
         ],
-        [ids, entered, *kernel1],
+        [*entered, *kernel1],
         flops=2 * 2176 * 27 * 128 * 256,
     )
-    part_peer = lax.ppermute(part_peer, "core", [(0, 1), (1, 0)])
-    parts = run(add_kernel, [shape(14, 48, 128)] * 4, [], [ids, part_own, part_peer])
+    part_peer = lax.ppermute(part_peer, "core", SWAP)
+    parts = run(add_kernel, [shape(14, 48, 128)] * 4, [], [part_own, part_peer])
     summands = [parts[0]] + [
         lax.ppermute(parts[n], ("xh", "tm"), [(i, i ^ n) for i in range(4)]) for n in (1, 2, 3)
     ]
-    second = run(middle_kernel, shape(9, 48, 384), [], [ids, *summands, vectors, cache_rows])
-    pair = lax.all_gather(second, "core", axis=0, tiled=True)
+    second = run(middle_kernel, shape(9, 48, 384), [], [*summands, vectors, cache_rows])
+    second, kernel2 = lax.optimization_barrier((second, kernel2))
+    other = lax.ppermute(second, "core", SWAP)
     own, peer = run(
         second_kernel,
         [shape(256, 256, dtype=F32), shape(256, 256, dtype=F32)],
@@ -431,11 +493,11 @@
             pltpu.VMEM((512, 256), F32),
             pltpu.VMEM((512, 256), F32),
         ],
-        [ids, pair, kernel2, bias2],
+        [second, other, kernel2, bias2],
         flops=2 * 512 * 27 * 384 * 256,
     )
-    peer = lax.ppermute(peer, "core", [(0, 1), (1, 0)])
-    return run(last_kernel, shape(4, 8, 8, 384), [pltpu.VMEM((3, 256, 128), F32)], [ids, own, peer, video])
+    peer = lax.ppermute(peer, "core", SWAP)
+    return run(last_kernel, shape(4, 8, 8, 384), [pltpu.VMEM((3, 256, 128), F32)], [own, peer, video])
 
 
 def solution(mesh):

time: 119 us -> 105 us (0.88)
  blocking collectives: 22.9 us -> 0 us
  starting transfers between devices: 26.4 us -> 42.1 us
  Pallas kernels: 20.9 us -> 18.3 us
  local copies, waits for them, and re-layouts: 7.61 us -> 5.49 us
  waiting for transfers between devices: 26.8 us -> 24.8 us
    ppermute x5 -> x15, starting transfers between devices: 4.3 us -> 25.9 us  [the longest x6 8.24 us: round_y(): lax.ppermute(x, 'y', [(i, (i + d) % 4) for i in range(4)])]
    all_to_all x1 -> x0, blocking collectives: 19.7 us -> none  [per_device(): near2 = lax.all_to_all(sent2, ('y', 'xh', 'core'), 0, 0)]
    all_to_all x1 -> x0, starting transfers between devices: 8.06 us -> none  [per_device(): entered = lax.all_to_all(entering, RING, 0, 0)]
    all_gather x1 -> x0, blocking collectives: 3.16 us -> none  [per_device(): pair = lax.all_gather(second, 'core', axis=0, tiled=True)]
    pallas_call x9 -> x12, Pallas kernels: 20.9 us -> 18.3 us  [run(): pl.pallas_call(kernel, out_shape=outs, in_specs=specs, out_specs=jax.tree...]
    ppermute x1, starting transfers between devices: 1.86 us -> 4.06 us  [per_device(): lax.ppermute(edges, LON, [(i, (i + 1) % 128 if i % 2 else (i - 1) % 128)...]
    unnamed x22 -> x16, local copies, waits for them, and re-layouts: 7.61 us -> 5.49 us
    ppermute x5 -> x15, waiting for transfers between devices: 15.3 us -> 14.5 us  [the longest x3 6.58 us: per_device(): lax.ppermute(v, ('xh', 'tm'), [(i, i ^ n) for i in range(4)])]
  transfers between devices with their start and end apart: 12 -> 21, of which waited for: 8 -> 14; matrix products, arithmetic and copies ran while one was open for 0% -> 0% of each run, Pallas kernels for 10% -> 11%
where the time goes in v2:
time: 105 us; the launch traced here: 104 us
  starting transfers between devices  42.1 us (40%)
  waiting for transfers between devices  24.8 us (24%)
  Pallas kernels  18.3 us (17%)
  between operations  13.5 us (13%)
  local copies, waits for them, and re-layouts  5.49 us (5%)
    pallas_call x12, Pallas kernels, run(): pl.pallas_call(kernel, out_shape=outs, in_specs=specs, out_specs=jax.tree...  18.3 us
    ppermute x3, waiting for transfers between devices, per_device(): lax.ppermute(parts[n], ('xh', 'tm'), [(i, i ^ n) for i in range(4)])  9.26 us
    ppermute x6, starting transfers between devices, round_y(): lax.ppermute(x, 'y', [(i, (i + d) % 4) for i in range(4)])  8.24 us
    all_to_all x1, starting transfers between devices, per_device(): near1 = lax.all_to_all(sent1, 'z', 0, 0)  8.2 us
    ppermute x3, waiting for transfers between devices, per_device(): lax.ppermute(v, ('xh', 'tm'), [(i, i ^ n) for i in range(4)])  6.58 us
    unnamed x16, local copies, waits for them, and re-layouts  5.49 us
    ppermute x1, starting transfers between devices, per_device(): part_peer = lax.ppermute(part_peer, 'core', SWAP)  5.17 us
    ppermute x1, starting transfers between devices, per_device(): lax.ppermute(edges, LON, [(i, (i + 1) % 128 if i % 2 else (i - 1) % 128)...  4.06 us
  transfers between devices with their start and end apart: 21, of which 14 were waited for; matrix products, arithmetic and copies ran while one was open for 0% of the time, Pallas kernels for 11%

profile of v2, /device:TPU:1, one launch (start us, length us, event | category | flops | bytes accessed | tf_op | source)
XLA Modules:
  0.0 104.2 jit_solution(17183427771337623807)
XLA Ops:
  6.5 1.8 %shard_map.91 = (bf16[124,128]{1,0:T(8,128)(2,1)}, bf16[124,128]{1,0:T(8,128)(2,1)}, bf16[96,384]{1,0:T(8,128)(2,1)}) custom-call(bf16[3,27,384]{2,1,0:T(8,128)(2,1)} %bitcast.9, bf16[4,8,8,384]{3,2,1,0:T(8,128)(2,1)} %video.5, bf16[2,8,8,384]{3,2,1,0:T(8,128)(2,1)} %cache1.3, bf16[2,8,8,384]{3,2,1,0:T(8,128)(2,1)} %cache2.3), custom_call_target="tpu_custom_call" | custom-call | bytes 455424 | tf_op jit(solution)/shard_map/pallas_call | solution.py:395
  8.4 3.2 %collective-permute-start = (bf16[124,128]{1,0:T(8,128)(2,1)}, bf16[124,128]{1,0:T(8,128)(2,1)S(1)}, u32[]{:S(2)}, u32[]{:S(2)}) collective-permute-start(bf16[124,128]{1,0:T(8,128)(2,1)} %get-tuple-element.35), channel_id=1, source_target_pairs={{0,2},{2,0},{1,3},{3,1},{4,6},{6,4},{5,7},{7,5},{8,10},{10,8},{9,1... | collective-permute-start | bytes 95240 | tf_op jit(solution)/shard_map/ppermute | solution.py:423
  14.5 2.8 %shard_map.93 = (bf16[8,124,128]{2,1,0:T(8,128)(2,1)}, bf16[4,320,128]{2,1,0:T(8,128)(2,1)}, bf16[8,16,384]{2,1,0:T(8,128)(2,1)}, f32[8,384]{1,0:T(8,128)}) custom-call(bf16[3,27,384]{2,1,0:T(8,128)(2,1)} %bitcast.10, bf16[4,8,8,384]{3,2,1,0:T(8,128)(2,1)} %video.5, bf16[2,8,8,384]{3,2,1,0:T(8,128)(2,1)} %cache1.3, bf16[2,8,8,384]{3,2,1,0:T(8,128)(2,1)} %cache2.3, ...), custom_call_target="tpu_custom_call" | custom-call | bytes 460032 | tf_op jit(solution)/shard_map/pallas_call | solution.py:395
  18.7 2.6 %collective-permute-start.3 = (bf16[4,124,128]{2,1,0:T(8,128)(2,1)S(1)}, bf16[4,124,128]{2,1,0:T(8,128)(2,1)S(1)}, u32[]{:S(2)}, u32[]{:S(2)}) collective-permute-start(bf16[4,124,128]{2,1,0:T(8,128)(2,1)S(1)} %bitcast.5), channel_id=1, source_target_pairs={{0,128},{64,192},{128,0},{192,64},{1,129},{65,193},{129,1},{193,65... | collective-permute-start | bytes 380936 | tf_op jit(solution)/shard_map/ppermute | solution.py:407
  22.4 4.1 %collective-permute-start.5 = (bf16[96,384]{1,0:T(8,128)(2,1)}, bf16[96,384]{1,0:T(8,128)(2,1)S(1)}, u32[]{:S(2)}, u32[]{:S(2)}) collective-permute-start(bf16[96,384]{1,0:T(8,128)(2,1)} %get-tuple-element.44), channel_id=1, source_target_pairs={{0,254},{2,4},{4,2},{6,8},{8,6},{10,12},{12,10},{14,16},{16,14},{1... | collective-permute-start | bytes 221192 | tf_op jit(solution)/shard_map/ppermute | solution.py:447
  27.1 1.7 %shard_map.95 = bf16[124,16,128]{2,1,0:T(8,128)(2,1)} custom-call(bf16[4,124,128]{2,1,0:T(8,128)(2,1)S(1)} %bitcast.7, bf16[4,124,128]{2,1,0:T(8,128)(2,1)S(1)} %collective-permute-done.2.w1, bf16[4,124,128]{2,1,0:T(8,128)(2,1)S(1)} %collective-permute-done.3.w2, bf16[4,124,128]{2,1,0:T(8,128)(2,1)S(1)} %collective-permute-done.4.w3), custom_call_target="tpu_custom_call" | custom-call | bytes 507904 | tf_op jit(solution)/shard_map/pallas_call | solution.py:395
  28.8 8.2 %all-to-all-start = ((bf16[8,124,128]{2,1,0:T(8,128)(2,1)}), bf16[8,124,128]{2,1,0:T(8,128)(2,1)S(1)}, u32[]{:S(2)}, u32[]{:S(2)}) async-start(bf16[8,124,128]{2,1,0:T(8,128)(2,1)} %get-tuple-element.50), calls=%async_computation | async-start | bytes 524288 | tf_op jit(solution)/shard_map/all_to_all | solution.py:450
  40.0 3.0 %collective-permute-start.6 = (bf16[2,400,128]{2,1,0:T(8,128)(2,1)S(1)}, bf16[2,400,128]{2,1,0:T(8,128)(2,1)S(1)}, u32[]{:S(2)}, u32[]{:S(2)}) collective-permute-start(bf16[2,400,128]{2,1,0:T(8,128)(2,1)S(1)} %get-tuple-element.47), channel_id=1, source_target_pairs={{0,2},{2,0},{1,3},{3,1},{4,6},{6,4},{5,7},{7,5},{8,10},{10,8},{9,1... | collective-permute-start | bytes 614408 | tf_op jit(solution)/shard_map/ppermute | solution.py:458
  44.1 1.3 %collective-permute-start.7 = (bf16[2,400,128]{2,1,0:T(8,128)(2,1)S(1)}, bf16[2,400,128]{2,1,0:T(8,128)(2,1)S(1)}, u32[]{:S(2)}, u32[]{:S(2)}) collective-permute-start(bf16[2,400,128]{2,1,0:T(8,128)(2,1)S(1)} %get-tuple-element.48.x0), channel_id=1, source_target_pairs={{0,1},{1,0},{4,5},{5,4},{2,3},{3,2},{6,7},{7,6},{8,9},{9,8},{12,13... | collective-permute-start | bytes 614408 | tf_op jit(solution)/shard_map/ppermute | solution.py:461
  47.6 2.8 %collective-permute-start.11 = (bf16[8,124,128]{2,1,0:T(8,128)(2,1)S(1)}, bf16[8,124,128]{2,1,0:T(8,128)(2,1)S(1)}, u32[]{:S(2)}, u32[]{:S(2)}) collective-permute-start(bf16[8,124,128]{2,1,0:T(8,128)(2,1)S(1)} %all-to-all-done.w0), channel_id=1, source_target_pairs={{0,128},{64,192},{128,0},{192,64},{1,129},{65,193},{129,1},{193,65... | collective-permute-start | bytes 761864 | tf_op jit(solution)/shard_map/ppermute | solution.py:407
  50.4 2.1 %collective-permute-start.8 = (bf16[2,400,128]{2,1,0:T(8,128)(2,1)S(1)}, bf16[2,400,128]{2,1,0:T(8,128)(2,1)S(1)}, u32[]{:S(2)}, u32[]{:S(2)}) collective-permute-start(bf16[2,400,128]{2,1,0:T(8,128)(2,1)S(1)} %get-tuple-element.49), channel_id=1, source_target_pairs={{0,4},{1,5},{4,0},{5,1},{2,6},{3,7},{6,2},{7,3},{8,12},{9,13},{12,... | collective-permute-start | bytes 614408 | tf_op jit(solution)/shard_map/ppermute | solution.py:461
  52.5 4.0 %collective-permute-done.8.x2 = bf16[2,400,128]{2,1,0:T(8,128)(2,1)S(1)} collective-permute-done((bf16[2,400,128]{2,1,0:T(8,128)(2,1)S(1)}, bf16[2,400,128]{2,1,0:T(8,128)(2,1)S(1)}, u32[]{:S(2)}, u32[]{:S(2)}) %collective-permute-start.8) | collective-permute-done | bytes 204832 | tf_op jit(solution)/shard_map/ppermute | solution.py:461
  56.6 2.5 %collective-permute-done.9.x3 = bf16[2,400,128]{2,1,0:T(8,128)(2,1)S(1)} collective-permute-done((bf16[2,400,128]{2,1,0:T(8,128)(2,1)S(1)}, bf16[2,400,128]{2,1,0:T(8,128)(2,1)S(1)}, u32[]{:S(2)}, u32[]{:S(2)}) %collective-permute-start.9) | collective-permute-done | bytes 204832 | tf_op jit(solution)/shard_map/ppermute | solution.py:461
  59.2 6.2 %shard_map.98 = (bf16[4,14,48,128]{3,2,1,0:T(8,128)(2,1)S(1)}, bf16[4,14,48,128]{3,2,1,0:T(8,128)(2,1)S(1)}) custom-call(bf16[2,400,128]{2,1,0:T(8,128)(2,1)S(1)} %get-tuple-element.48.x0, bf16[2,400,128]{2,1,0:T(8,128)(2,1)S(1)} %collective-permute-done.7.x1, bf16[2,400,128]{2,1,0:T(8,128)(2,1)S(1)} %collective-permute-done.8.x2, ...), custom_call_target="tpu_custom_call" | custom-call | flops 3850371072 | bytes 1835008 | tf_op jit(solution)/shard_map/pallas_call | solution.py:395
  65.4 5.2 %collective-permute-start.13 = (bf16[4,14,48,128]{3,2,1,0:T(8,128)(2,1)S(1)}, bf16[4,14,48,128]{3,2,1,0:T(8,128)(2,1)S(1)}, u32[]{:S(2)}, u32[]{:S(2)}) collective-permute-start(bf16[4,14,48,128]{3,2,1,0:T(8,128)(2,1)S(1)} %get-tuple-element.52), channel_id=1, source_target_pairs={{0,2},{2,0},{1,3},{3,1},{4,6},{6,4},{5,7},{7,5},{8,10},{10,8},{9,1... | collective-permute-start | bytes 2064392 | tf_op jit(solution)/shard_map/ppermute | solution.py:479
  70.6 1.8 %collective-permute-done.13.y = bf16[4,14,48,128]{3,2,1,0:T(8,128)(2,1)S(1)} collective-permute-done((bf16[4,14,48,128]{3,2,1,0:T(8,128)(2,1)S(1)}, bf16[4,14,48,128]{3,2,1,0:T(8,128)(2,1)S(1)}, u32[]{:S(2)}, u32[]{:S(2)}) %collective-permute-start.13) | collective-permute-done | bytes 688160 | tf_op jit(solution)/shard_map/ppermute | solution.py:479
  73.3 2.0 %collective-permute-start.15 = (bf16[14,48,128]{2,1,0:T(8,128)(2,1)S(1)}, bf16[14,48,128]{2,1,0:T(8,128)(2,1)S(1)}, u32[]{:S(2)}, u32[]{:S(2)}) collective-permute-start(bf16[14,48,128]{2,1,0:T(8,128)(2,1)S(1)} %get-tuple-element.55), channel_id=1, source_target_pairs={{0,4},{1,5},{4,0},{5,1},{2,6},{3,7},{6,2},{7,3},{8,12},{9,13},{12,... | collective-permute-start | bytes 516104 | tf_op jit(solution)/shard_map/ppermute | solution.py:482
  75.3 1.3 %collective-permute-start.16 = (bf16[14,48,128]{2,1,0:T(8,128)(2,1)S(1)}, bf16[14,48,128]{2,1,0:T(8,128)(2,1)S(1)}, u32[]{:S(2)}, u32[]{:S(2)}) collective-permute-start(bf16[14,48,128]{2,1,0:T(8,128)(2,1)S(1)} %get-tuple-element.56), channel_id=1, source_target_pairs={{0,5},{1,4},{4,1},{5,0},{2,7},{3,6},{6,3},{7,2},{8,13},{9,12},{12,... | collective-permute-start | bytes 516104 | tf_op jit(solution)/shard_map/ppermute | solution.py:482
  76.6 1.8 %collective-permute-done.14.x1 = bf16[14,48,128]{2,1,0:T(8,128)(2,1)S(1)} collective-permute-done((bf16[14,48,128]{2,1,0:T(8,128)(2,1)S(1)}, bf16[14,48,128]{2,1,0:T(8,128)(2,1)S(1)}, u32[]{:S(2)}, u32[]{:S(2)}) %collective-permute-start.14) | collective-permute-done | bytes 172064 | tf_op jit(solution)/shard_map/ppermute | solution.py:482
  78.4 4.7 %collective-permute-done.15.x2 = bf16[14,48,128]{2,1,0:T(8,128)(2,1)S(1)} collective-permute-done((bf16[14,48,128]{2,1,0:T(8,128)(2,1)S(1)}, bf16[14,48,128]{2,1,0:T(8,128)(2,1)S(1)}, u32[]{:S(2)}, u32[]{:S(2)}) %collective-permute-start.15) | collective-permute-done | bytes 172064 | tf_op jit(solution)/shard_map/ppermute | solution.py:482
  83.2 2.7 %collective-permute-done.16.x3 = bf16[14,48,128]{2,1,0:T(8,128)(2,1)S(1)} collective-permute-done((bf16[14,48,128]{2,1,0:T(8,128)(2,1)S(1)}, bf16[14,48,128]{2,1,0:T(8,128)(2,1)S(1)}, u32[]{:S(2)}, u32[]{:S(2)}) %collective-permute-start.16) | collective-permute-done | bytes 172064 | tf_op jit(solution)/shard_map/ppermute | solution.py:482
  87.6 1.3 %collective-permute-done.17.other = bf16[9,48,384]{2,1,0:T(8,128)(2,1)S(1)} collective-permute-done((bf16[9,48,384]{2,1,0:T(8,128)(2,1)S(1)}, bf16[9,48,384]{2,1,0:T(8,128)(2,1)S(1)}, u32[]{:S(2)}, u32[]{:S(2)}) %collective-permute-start.17) | collective-permute-done | bytes 331808 | tf_op jit(solution)/shard_map/ppermute | solution.py:486
  88.9 2.1 %copy-done.6 = bf16[992,16,128]{2,1,0:T(8,128)(2,1)S(1)} copy-done((bf16[992,16,128]{2,1,0:T(8,128)(2,1)S(1)}, bf16[992,16,128]{2,1,0:T(8,128)(2,1)}, u32[]{:S(2)}) %copy-start.6) | copy-done | bytes 4063256
  91.0 3.6 %shard_map.101 = (f32[256,256]{1,0:T(8,128)S(1)}, f32[256,256]{1,0:T(8,128)S(1)}) custom-call(bf16[9,48,384]{2,1,0:T(8,128)(2,1)S(1)} %shard_map.100.mine, bf16[9,48,384]{2,1,0:T(8,128)(2,1)S(1)} %collective-permute-done.17.other, bf16[8,124,16,128]{3,2,1,0:T(8,128)(2,1)S(1)} %bitcast.8, f32[384]{0:T(512)S(1)} %copy-done.7), custom_call_target="tpu_custom_call" | custom-call | flops 2717908992 | bytes 4728320 | tf_op jit(solution)/shard_map/pallas_call | solution.py:395
  (47 shorter events, 17.8 us)
Async XLA Ops:
  6.5 79.9 %all-gather.3.cloned.1.call-start = ((), (), s32[]{:S(2)}) async-start(), calls=%async_computation.1 | async-start | bytes 4571136 | tf_op jit(solution)/shard_map/all_gather | solution.py:451
  8.4 4.3 %collective-permute-start = (bf16[124,128]{1,0:T(8,128)(2,1)}, bf16[124,128]{1,0:T(8,128)(2,1)S(1)}, u32[]{:S(2)}, u32[]{:S(2)}) collective-permute-start(bf16[124,128]{1,0:T(8,128)(2,1)} %get-tuple-element.35), channel_id=1, source_target_pairs={{0,2},{2,0},{1,3},{3,1},{4,6},{6,4},{5,7},{7,5},{8,10},{10,8},{9,1... | collective-permute-start | bytes 95240 | tf_op jit(solution)/shard_map/ppermute | solution.py:423
  13.5 4.7 %collective-permute-start.1 = (bf16[2,124,128]{2,1,0:T(8,128)(2,1)S(1)}, bf16[2,124,128]{2,1,0:T(8,128)(2,1)S(1)}, u32[]{:S(2)}, u32[]{:S(2)}) collective-permute-start(bf16[2,124,128]{2,1,0:T(8,128)(2,1)S(1)} %shard_map.92.mine), channel_id=1, source_target_pairs={{0,4},{4,0},{1,5},{5,1},{2,6},{6,2},{3,7},{7,3},{8,12},{12,8},{9,1... | collective-permute-start | bytes 190472 | tf_op jit(solution)/shard_map/ppermute | solution.py:442
  18.2 8.3 %collective-permute-start.2 = (bf16[4,124,128]{2,1,0:T(8,128)(2,1)S(1)}, bf16[4,124,128]{2,1,0:T(8,128)(2,1)S(1)}, u32[]{:S(2)}, u32[]{:S(2)}) collective-permute-start(bf16[4,124,128]{2,1,0:T(8,128)(2,1)S(1)} %bitcast.4), channel_id=1, source_target_pairs={{0,64},{64,128},{128,192},{192,0},{1,65},{65,129},{129,193},{193,1... | collective-permute-start | bytes 380936 | tf_op jit(solution)/shard_map/ppermute | solution.py:407
  18.7 8.4 %collective-permute-start.3 = (bf16[4,124,128]{2,1,0:T(8,128)(2,1)S(1)}, bf16[4,124,128]{2,1,0:T(8,128)(2,1)S(1)}, u32[]{:S(2)}, u32[]{:S(2)}) collective-permute-start(bf16[4,124,128]{2,1,0:T(8,128)(2,1)S(1)} %bitcast.5), channel_id=1, source_target_pairs={{0,128},{64,192},{128,0},{192,64},{1,129},{65,193},{129,1},{193,65... | collective-permute-start | bytes 380936 | tf_op jit(solution)/shard_map/ppermute | solution.py:407
  21.3 5.8 %collective-permute-start.4 = (bf16[4,124,128]{2,1,0:T(8,128)(2,1)S(1)}, bf16[4,124,128]{2,1,0:T(8,128)(2,1)S(1)}, u32[]{:S(2)}, u32[]{:S(2)}) collective-permute-start(bf16[4,124,128]{2,1,0:T(8,128)(2,1)S(1)} %bitcast.6), channel_id=1, source_target_pairs={{0,192},{64,0},{128,64},{192,128},{1,193},{65,1},{129,65},{193,129... | collective-permute-start | bytes 380936 | tf_op jit(solution)/shard_map/ppermute | solution.py:407
  22.4 6.4 %collective-permute-start.5 = (bf16[96,384]{1,0:T(8,128)(2,1)}, bf16[96,384]{1,0:T(8,128)(2,1)S(1)}, u32[]{:S(2)}, u32[]{:S(2)}) collective-permute-start(bf16[96,384]{1,0:T(8,128)(2,1)} %get-tuple-element.44), channel_id=1, source_target_pairs={{0,254},{2,4},{4,2},{6,8},{8,6},{10,12},{12,10},{14,16},{16,14},{1... | collective-permute-start | bytes 221192 | tf_op jit(solution)/shard_map/ppermute | solution.py:447
  28.8 17.6 %all-to-all-start = ((bf16[8,124,128]{2,1,0:T(8,128)(2,1)}), bf16[8,124,128]{2,1,0:T(8,128)(2,1)S(1)}, u32[]{:S(2)}, u32[]{:S(2)}) async-start(bf16[8,124,128]{2,1,0:T(8,128)(2,1)} %get-tuple-element.50), calls=%async_computation | async-start | bytes 524288 | tf_op jit(solution)/shard_map/all_to_all | solution.py:450
  40.0 4.1 %collective-permute-start.6 = (bf16[2,400,128]{2,1,0:T(8,128)(2,1)S(1)}, bf16[2,400,128]{2,1,0:T(8,128)(2,1)S(1)}, u32[]{:S(2)}, u32[]{:S(2)}) collective-permute-start(bf16[2,400,128]{2,1,0:T(8,128)(2,1)S(1)} %get-tuple-element.47), channel_id=1, source_target_pairs={{0,2},{2,0},{1,3},{3,1},{4,6},{6,4},{5,7},{7,5},{8,10},{10,8},{9,1... | collective-permute-start | bytes 614408 | tf_op jit(solution)/shard_map/ppermute | solution.py:458
  44.1 8.4 %collective-permute-start.7 = (bf16[2,400,128]{2,1,0:T(8,128)(2,1)S(1)}, bf16[2,400,128]{2,1,0:T(8,128)(2,1)S(1)}, u32[]{:S(2)}, u32[]{:S(2)}) collective-permute-start(bf16[2,400,128]{2,1,0:T(8,128)(2,1)S(1)} %get-tuple-element.48.x0), channel_id=1, source_target_pairs={{0,1},{1,0},{4,5},{5,4},{2,3},{3,2},{6,7},{7,6},{8,9},{9,8},{12,13... | collective-permute-start | bytes 614408 | tf_op jit(solution)/shard_map/ppermute | solution.py:461
  46.4 12.7 %collective-permute-start.10 = (bf16[8,124,128]{2,1,0:T(8,128)(2,1)S(1)}, bf16[8,124,128]{2,1,0:T(8,128)(2,1)S(1)}, u32[]{:S(2)}, u32[]{:S(2)}) collective-permute-start(bf16[8,124,128]{2,1,0:T(8,128)(2,1)S(1)} %all-to-all-done.w0), channel_id=1, source_target_pairs={{0,64},{64,128},{128,192},{192,0},{1,65},{65,129},{129,193},{193,1... | collective-permute-start | bytes 761864 | tf_op jit(solution)/shard_map/ppermute | solution.py:407
  47.6 11.7 %collective-permute-start.11 = (bf16[8,124,128]{2,1,0:T(8,128)(2,1)S(1)}, bf16[8,124,128]{2,1,0:T(8,128)(2,1)S(1)}, u32[]{:S(2)}, u32[]{:S(2)}) collective-permute-start(bf16[8,124,128]{2,1,0:T(8,128)(2,1)S(1)} %all-to-all-done.w0), channel_id=1, source_target_pairs={{0,128},{64,192},{128,0},{192,64},{1,129},{65,193},{129,1},{193,65... | collective-permute-start | bytes 761864 | tf_op jit(solution)/shard_map/ppermute | solution.py:407
  50.4 8.8 %collective-permute-start.12 = (bf16[8,124,128]{2,1,0:T(8,128)(2,1)S(1)}, bf16[8,124,128]{2,1,0:T(8,128)(2,1)S(1)}, u32[]{:S(2)}, u32[]{:S(2)}) collective-permute-start(bf16[8,124,128]{2,1,0:T(8,128)(2,1)S(1)} %all-to-all-done.w0), channel_id=1, source_target_pairs={{0,192},{64,0},{128,64},{192,128},{1,193},{65,1},{129,65},{193,129... | collective-permute-start | bytes 761864 | tf_op jit(solution)/shard_map/ppermute | solution.py:407
  50.4 35.5 %copy-start.4 = (f32[8,384]{1,0:T(8,128)S(1)}, f32[8,384]{1,0:T(8,128)}, u32[]{:S(2)}) copy-start(f32[8,384]{1,0:T(8,128)} %get-tuple-element.39.vec) | copy-start | bytes 36868
  50.4 38.5 %copy-start.7 = (f32[384]{0:T(512)S(1)}, f32[384]{0:T(512)}, u32[]{:S(2)}) copy-start(f32[384]{0:T(512)} %bias.1) | copy-start | bytes 4612
  50.4 6.2 %collective-permute-start.8 = (bf16[2,400,128]{2,1,0:T(8,128)(2,1)S(1)}, bf16[2,400,128]{2,1,0:T(8,128)(2,1)S(1)}, u32[]{:S(2)}, u32[]{:S(2)}) collective-permute-start(bf16[2,400,128]{2,1,0:T(8,128)(2,1)S(1)} %get-tuple-element.49), channel_id=1, source_target_pairs={{0,4},{1,5},{4,0},{5,1},{2,6},{3,7},{6,2},{7,3},{8,12},{9,13},{12,... | collective-permute-start | bytes 614408 | tf_op jit(solution)/shard_map/ppermute | solution.py:461
  52.5 6.6 %collective-permute-start.9 = (bf16[2,400,128]{2,1,0:T(8,128)(2,1)S(1)}, bf16[2,400,128]{2,1,0:T(8,128)(2,1)S(1)}, u32[]{:S(2)}, u32[]{:S(2)}) collective-permute-start(bf16[2,400,128]{2,1,0:T(8,128)(2,1)S(1)} %get-tuple-element.49), channel_id=1, source_target_pairs={{0,5},{1,4},{4,1},{5,0},{2,7},{3,6},{6,3},{7,2},{8,13},{9,12},{12,... | collective-permute-start | bytes 614408 | tf_op jit(solution)/shard_map/ppermute | solution.py:461
  65.4 6.9 %collective-permute-start.13 = (bf16[4,14,48,128]{3,2,1,0:T(8,128)(2,1)S(1)}, bf16[4,14,48,128]{3,2,1,0:T(8,128)(2,1)S(1)}, u32[]{:S(2)}, u32[]{:S(2)}) collective-permute-start(bf16[4,14,48,128]{3,2,1,0:T(8,128)(2,1)S(1)} %get-tuple-element.52), channel_id=1, source_target_pairs={{0,2},{2,0},{1,3},{3,1},{4,6},{6,4},{5,7},{7,5},{8,10},{10,8},{9,1... | collective-permute-start | bytes 2064392 | tf_op jit(solution)/shard_map/ppermute | solution.py:479
  72.7 5.8 %collective-permute-start.14 = (bf16[14,48,128]{2,1,0:T(8,128)(2,1)S(1)}, bf16[14,48,128]{2,1,0:T(8,128)(2,1)S(1)}, u32[]{:S(2)}, u32[]{:S(2)}) collective-permute-start(bf16[14,48,128]{2,1,0:T(8,128)(2,1)S(1)} %get-tuple-element.54), channel_id=1, source_target_pairs={{0,1},{1,0},{4,5},{5,4},{2,3},{3,2},{6,7},{7,6},{8,9},{9,8},{12,13... | collective-permute-start | bytes 516104 | tf_op jit(solution)/shard_map/ppermute | solution.py:482
  73.3 9.8 %collective-permute-start.15 = (bf16[14,48,128]{2,1,0:T(8,128)(2,1)S(1)}, bf16[14,48,128]{2,1,0:T(8,128)(2,1)S(1)}, u32[]{:S(2)}, u32[]{:S(2)}) collective-permute-start(bf16[14,48,128]{2,1,0:T(8,128)(2,1)S(1)} %get-tuple-element.55), channel_id=1, source_target_pairs={{0,4},{1,5},{4,0},{5,1},{2,6},{3,7},{6,2},{7,3},{8,12},{9,13},{12,... | collective-permute-start | bytes 516104 | tf_op jit(solution)/shard_map/ppermute | solution.py:482
  75.3 10.5 %collective-permute-start.16 = (bf16[14,48,128]{2,1,0:T(8,128)(2,1)S(1)}, bf16[14,48,128]{2,1,0:T(8,128)(2,1)S(1)}, u32[]{:S(2)}, u32[]{:S(2)}) collective-permute-start(bf16[14,48,128]{2,1,0:T(8,128)(2,1)S(1)} %get-tuple-element.56), channel_id=1, source_target_pairs={{0,5},{1,4},{4,1},{5,0},{2,7},{3,6},{6,3},{7,2},{8,13},{9,12},{12,... | collective-permute-start | bytes 516104 | tf_op jit(solution)/shard_map/ppermute | solution.py:482
  86.4 9.9 %copy-start = (bf16[4,8,8,384]{3,2,1,0:T(8,128)(2,1)S(1)}, bf16[4,8,8,384]{3,2,1,0:T(8,128)(2,1)}, u32[]{:S(2)}) copy-start(bf16[4,8,8,384]{3,2,1,0:T(8,128)(2,1)} %video.5) | copy-start | bytes 589828
  86.4 2.5 %collective-permute-start.17 = (bf16[9,48,384]{2,1,0:T(8,128)(2,1)S(1)}, bf16[9,48,384]{2,1,0:T(8,128)(2,1)S(1)}, u32[]{:S(2)}, u32[]{:S(2)}) collective-permute-start(bf16[9,48,384]{2,1,0:T(8,128)(2,1)S(1)} %shard_map.100.mine), channel_id=1, source_target_pairs={{0,2},{2,0},{1,3},{3,1},{4,6},{6,4},{5,7},{7,5},{8,10},{10,8},{9,1... | collective-permute-start | bytes 995336 | tf_op jit(solution)/shard_map/ppermute | solution.py:486
  94.7 1.6 %collective-permute-start.18 = (f32[256,256]{1,0:T(8,128)S(1)}, f32[256,256]{1,0:T(8,128)S(1)}, u32[]{:S(2)}, u32[]{:S(2)}) collective-permute-start(f32[256,256]{1,0:T(8,128)S(1)} %get-tuple-element.62), channel_id=1, source_target_pairs={{0,2},{2,0},{1,3},{3,1},{4,6},{6,4},{5,7},{7,5},{8,10},{10,8},{9,1... | collective-permute-start | bytes 786440 | tf_op jit(solution)/shard_map/ppermute | solution.py:499
  (5 other events, 5.5 us)
Sparse Core Ops, SparseCore 0:
  28.9 57.4 all-gather.2

commit v3 on v2

--- a/solution.py
+++ b/solution.py
@@ -74,7 +74,22 @@
 def by_slice(x, gain):
     frame = lax.rem(lax.broadcasted_iota(jnp.int32, x.shape, 0) >> 3, 5)
     x = jnp.where(frame == 4, x, norm_silu(x, gain)).astype(BF16)
-    return jnp.dot(x, spread_matrix().astype(BF16), preferred_element_type=F32).astype(BF16)
+    return jnp.dot(x, spread_matrix().astype(BF16), preferred_element_type=F32)
+
+
+def squeezed(x):
+    free = lanes((80, 128)) >= 96
+    kept = [jnp.where(free, pltpu.roll(x[240:], 96 - 32 * k, 1), x[80 * k : 80 * k + 80]) for k in range(3)]
+    return jnp.concatenate(kept, axis=0)
+
+
+def stretched(x):
+    lane = lanes((80, 128))
+    parts = [x[80 * k : 80 * k + 80] for k in range(3)]
+    last = jnp.zeros((80, 128), F32)
+    for k in range(3):
+        last = jnp.where(lane >> 5 == k, pltpu.roll(parts[k], 32 + 32 * k, 1), last)
+    return jnp.concatenate([jnp.where(lane < 96, part, 0.0) for part in parts] + [last], axis=0)
 
 
 def ordered(x):
@@ -126,7 +141,7 @@
             rows[at : at + 8] = every(wide, 64 * f + c, 8)
     slices = by_slice(rows[...], gain1[...].reshape(1, 384))
     for q in range(4):
-        out[q] = slices[:, 128 * q : 128 * q + 128]
+        out[q] = squeezed(slices[:, 128 * q : 128 * q + 128]).astype(BF16)
     for c in range(8):
         for f in range(2):
             at = 16 * c + 8 * f
@@ -160,26 +175,16 @@
     lax.fori_loop(0, 124, step, 0, unroll=4)
 
 
-def enter_kernel(own, cache, vec, halo, keep, give, out_cache, edge):
-    ids = position()
-    slices = by_slice(halo[0:80].astype(F32), vec[2:3])
+def enter_kernel(own, gain, halo, keep, give, out_cache, edge):
+    ids = position()
+    slices = by_slice(halo[0:80].astype(F32), gain[...].reshape(1, 384))
     for q in range(4):
-        edge[q] = slices[:, 128 * q : 128 * q + 128]
+        edge[q] = slices[:, 128 * q : 128 * q + 128].astype(BF16)
     for xh in range(2):
         for out, core in ((keep, ids[0]), (give, 1 - ids[0])):
-            out[xh, 0:320] = own[2 * xh + core]
-            out[xh, 320:400] = edge[2 * xh + core]
-    beyond = ordered(halo[80:96])
-
-    @pl.when(ids[0] == 0)
-    def _():
-        out_cache[0] = beyond
-        out_cache[1:9] = cache[...]
-
-    @pl.when(ids[0] == 1)
-    def _():
-        out_cache[0:8] = cache[...]
-        out_cache[8] = beyond
+            out[xh, 0:240] = own[2 * xh + core]
+            out[xh, 240:320] = edge[2 * xh + core]
+    out_cache[...] = ordered(halo[80:96])
 
 
 def arrange_kernel(keep, got, same, across):
@@ -204,13 +209,14 @@
     return t // 9, (t // 3) % 3, t % 3
 
 
-def first_kernel(x0, x1, x2, x3, w0, w1, w2, w3, out_own, out_peer, field, even, odd, wide, kernel, part_a, part_b):
+def field_kernel(x0, x1, x2, x3, even, odd, field):
     ids = position()
     for n, x in enumerate((x0, x1, x2, x3)):
         tm = ids[1] ^ (n & 1)
         for m in range(2):
             q = 2 * (ids[2] ^ (n >> 1)) + (ids[0] ^ m)
-            piece = x[m].astype(F32).reshape(10, 5, 8, 128)
+            packed = x[m].astype(F32)
+            piece = jnp.concatenate([stretched(packed[:240]), packed[240:]], axis=0).reshape(10, 5, 8, 128)
 
             def place(at, begin, end):
                 field[pl.ds(at, end - begin), pl.ds(2 + 4 * tm, 4)] = piece[begin:end, 0:4]
@@ -230,6 +236,9 @@
 
     lax.fori_loop(0, 36, spread, 0, unroll=4)
 
+
+def first_kernel(even, odd, w0, w1, w2, w3, out_own, out_peer, wide, kernel, part_a, part_b):
+    ids = position()
     for d, w in enumerate((w0, w1, w2, w3)):
         at = pl.multiple_of(1024 * ((ids[3] + 4 - d) & 3), 1024)
         for z in range(8):
@@ -300,10 +309,16 @@
         lax.fori_loop(0, 14, step, 0, unroll=2)
 
 
-def middle_kernel(x0, x1, x2, x3, vec, cache, out):
+def middle_kernel(x0, x1, x2, x3, vec, cache, beyond, out):
     ids = position()
     low_lanes = lanes((48, 128)) < 64
     starts = ids[1] == 0
+
+    def cached(c):
+        low = beyond[...] if c == 0 else cache[c - 1]
+        high = beyond[...] if c == 8 else cache[c]
+        return jnp.where(ids[0] == 0, low, high)
+
     bias, gain = vec[0:1], vec[1:2]
 
     def summed(tm, j):
@@ -320,7 +335,7 @@
             hidden = jnp.concatenate([summed(0, c), summed(1, c), b], axis=1) + bias
             normed = norm_silu(hidden, gain).astype(BF16)
             out[c, 16:48] = normed[16:48]
-            out[c, 0:16] = jnp.where(starts, cache[c], normed[0:16])
+            out[c, 0:16] = jnp.where(starts, cached(c), normed[0:16])
 
 
 def second_kernel(mine, other, w, bias, out_own, out_peer, even, odd, low, high):
@@ -427,7 +442,7 @@
         send_kernel,
         [
             shape(8, 124, 128),
-            shape(4, 320, 128),
+            shape(4, 240, 128),
             shape(8, 16, 384),
             shape(8, 384, dtype=F32),
         ],
@@ -449,40 +464,44 @@
     sent1, turned2, halo = lax.optimization_barrier((sent1, turned2, halo))
     near1 = lax.all_to_all(sent1, "z", 0, 0)
     kernel2 = lax.all_gather(turned2, "z", axis=0, tiled=False)
-    keep, give, cache_rows = run(
+    keep, give, beyond = run(
         enter_kernel,
-        [shape(2, 400, 128), shape(2, 400, 128), shape(9, 16, 384)],
+        [shape(2, 320, 128), shape(2, 320, 128), shape(16, 384)],
         [pltpu.VMEM((4, 80, 128), BF16)],
-        [slices, cache_own, vectors, halo],
+        [slices, gain1, halo],
     )
     got = lax.ppermute(give, "core", SWAP)
-    same, across = run(arrange_kernel, [shape(2, 400, 128)] * 2, [], [keep, got])
+    same, across = run(arrange_kernel, [shape(2, 320, 128)] * 2, [], [keep, got])
     entered = [same] + [
         lax.ppermute(v, ("xh", "tm"), [(i, i ^ n) for i in range(4)]) for n, v in ((1, same), (2, across), (3, across))
     ]
     kernel1 = [near1, *round_y(near1)]
+    even, odd = run(
+        field_kernel,
+        [shape(3, 36, 80, 128), shape(3, 36, 64, 128)],
+        [pltpu.VMEM((36, 10, 8, 128), F32)],
+        entered,
+        limit=40,
+    )
     part_own, part_peer = run(
         first_kernel,
         [shape(4, 14, 48, 128), shape(4, 14, 48, 128)],
         [
-            pltpu.VMEM((36, 10, 8, 128), F32),
-            pltpu.VMEM((3, 36, 80, 128), BF16),
-            pltpu.VMEM((3, 36, 64, 128), BF16),
             pltpu.VMEM((4096, 128), F32),
             pltpu.VMEM((27, 128, 256), BF16),
             pltpu.VMEM((34, 64, 128), F32),
             pltpu.VMEM((34, 64, 128), F32),
         ],
-        [*entered, *kernel1],
+        [even, odd, *kernel1],
         flops=2 * 2176 * 27 * 128 * 256,
+        limit=40,
     )
     part_peer = lax.ppermute(part_peer, "core", SWAP)
     parts = run(add_kernel, [shape(14, 48, 128)] * 4, [], [part_own, part_peer])
     summands = [parts[0]] + [
         lax.ppermute(parts[n], ("xh", "tm"), [(i, i ^ n) for i in range(4)]) for n in (1, 2, 3)
     ]
-    second = run(middle_kernel, shape(9, 48, 384), [], [*summands, vectors, cache_rows])
-    second, kernel2 = lax.optimization_barrier((second, kernel2))
+    second = run(middle_kernel, shape(9, 48, 384), [], [*summands, vectors, cache_own, beyond])
     other = lax.ppermute(second, "core", SWAP)
     own, peer = run(
         second_kernel,

time: 105 us -> 104 us (level)
  local copies, waits for them, and re-layouts: 5.49 us -> 2.94 us
  waiting for transfers between devices: 24.8 us -> 26.4 us
    all_to_all x1, waiting for transfers between devices: 1.02 us -> 3.7 us  [per_device(): near1 = lax.all_to_all(sent1, 'z', 0, 0)]
    unnamed x16, local copies, waits for them, and re-layouts: 5.49 us -> 2.94 us
    pallas_call x12 -> x13, Pallas kernels: 18.3 us -> 18.8 us  [run(): pl.pallas_call(kernel, out_shape=outs, in_specs=specs, out_specs=jax.tree...]
  transfers between devices with their start and end apart: 21 -> 21, of which waited for: 14 -> 13; matrix products, arithmetic and copies ran while one was open for 0% -> 0% of each run, Pallas kernels for 11% -> 12%
where the time goes in v3:
time: 104 us
  starting transfers between devices  42 us (40%)
  waiting for transfers between devices  26.4 us (25%)
  Pallas kernels  18.8 us (18%)
  between operations  13.5 us (13%)
  local copies, waits for them, and re-layouts  2.94 us (3%)
    pallas_call x13, Pallas kernels, run(): pl.pallas_call(kernel, out_shape=outs, in_specs=specs, out_specs=jax.tree...  18.8 us
    ppermute x3, waiting for transfers between devices, per_device(): lax.ppermute(parts[n], ('xh', 'tm'), [(i, i ^ n) for i in range(4)])  9.13 us
    ppermute x6, starting transfers between devices, round_y(): lax.ppermute(x, 'y', [(i, (i + d) % 4) for i in range(4)])  8.29 us
    all_to_all x1, starting transfers between devices, per_device(): near1 = lax.all_to_all(sent1, 'z', 0, 0)  8.2 us
    ppermute x3, waiting for transfers between devices, per_device(): lax.ppermute(v, ('xh', 'tm'), [(i, i ^ n) for i in range(4)])  5.78 us
    ppermute x1, starting transfers between devices, per_device(): part_peer = lax.ppermute(part_peer, 'core', SWAP)  5.21 us
    ppermute x1, starting transfers between devices, per_device(): lax.ppermute(edges, LON, [(i, (i + 1) % 128 if i % 2 else (i - 1) % 128)...  4.02 us
    ppermute x3, starting transfers between devices, per_device(): lax.ppermute(parts[n], ('xh', 'tm'), [(i, i ^ n) for i in range(4)])  3.95 us
  transfers between devices with their start and end apart: 21, of which 13 were waited for; matrix products, arithmetic and copies ran while one was open for 0% of the time, Pallas kernels for 12%

profile of v3, /device:TPU:1, one launch (start us, length us, event | category | flops | bytes accessed | tf_op | source)
XLA Modules:
  0.0 103.7 jit_solution(10061106180727037781)
XLA Ops:
  6.5 1.8 %shard_map.91 = (bf16[124,128]{1,0:T(8,128)(2,1)}, bf16[124,128]{1,0:T(8,128)(2,1)}, bf16[96,384]{1,0:T(8,128)(2,1)}) custom-call(bf16[3,27,384]{2,1,0:T(8,128)(2,1)} %bitcast.9, bf16[4,8,8,384]{3,2,1,0:T(8,128)(2,1)} %video.5, bf16[2,8,8,384]{3,2,1,0:T(8,128)(2,1)} %cache1.3, bf16[2,8,8,384]{3,2,1,0:T(8,128)(2,1)} %cache2.3), custom_call_target="tpu_custom_call" | custom-call | bytes 455424 | tf_op jit(solution)/shard_map/pallas_call | solution.py:410
  8.4 3.2 %collective-permute-start = (bf16[124,128]{1,0:T(8,128)(2,1)}, bf16[124,128]{1,0:T(8,128)(2,1)S(1)}, u32[]{:S(2)}, u32[]{:S(2)}) collective-permute-start(bf16[124,128]{1,0:T(8,128)(2,1)} %get-tuple-element.35), channel_id=1, source_target_pairs={{0,2},{2,0},{1,3},{3,1},{4,6},{6,4},{5,7},{7,5},{8,10},{10,8},{9,1... | collective-permute-start | bytes 95240 | tf_op jit(solution)/shard_map/ppermute | solution.py:438
  14.6 2.8 %shard_map.93 = (bf16[8,124,128]{2,1,0:T(8,128)(2,1)}, bf16[4,240,128]{2,1,0:T(8,128)(2,1)}, bf16[8,16,384]{2,1,0:T(8,128)(2,1)}, f32[8,384]{1,0:T(8,128)}) custom-call(bf16[3,27,384]{2,1,0:T(8,128)(2,1)} %bitcast.10, bf16[4,8,8,384]{3,2,1,0:T(8,128)(2,1)} %video.5, bf16[2,8,8,384]{3,2,1,0:T(8,128)(2,1)} %cache1.3, bf16[2,8,8,384]{3,2,1,0:T(8,128)(2,1)} %cache2.3, ...), custom_call_target="tpu_custom_call" | custom-call | bytes 460032 | tf_op jit(solution)/shard_map/pallas_call | solution.py:410
  18.8 2.6 %collective-permute-start.3 = (bf16[4,124,128]{2,1,0:T(8,128)(2,1)S(1)}, bf16[4,124,128]{2,1,0:T(8,128)(2,1)S(1)}, u32[]{:S(2)}, u32[]{:S(2)}) collective-permute-start(bf16[4,124,128]{2,1,0:T(8,128)(2,1)S(1)} %bitcast.5), channel_id=1, source_target_pairs={{0,128},{64,192},{128,0},{192,64},{1,129},{65,193},{129,1},{193,65... | collective-permute-start | bytes 380936 | tf_op jit(solution)/shard_map/ppermute | solution.py:422
  22.5 4.0 %collective-permute-start.5 = (bf16[96,384]{1,0:T(8,128)(2,1)}, bf16[96,384]{1,0:T(8,128)(2,1)S(1)}, u32[]{:S(2)}, u32[]{:S(2)}) collective-permute-start(bf16[96,384]{1,0:T(8,128)(2,1)} %get-tuple-element.42), channel_id=1, source_target_pairs={{0,254},{2,4},{4,2},{6,8},{8,6},{10,12},{12,10},{14,16},{16,14},{1... | collective-permute-start | bytes 221192 | tf_op jit(solution)/shard_map/ppermute | solution.py:462
  27.2 1.7 %shard_map.95 = bf16[124,16,128]{2,1,0:T(8,128)(2,1)} custom-call(bf16[4,124,128]{2,1,0:T(8,128)(2,1)S(1)} %bitcast.7, bf16[4,124,128]{2,1,0:T(8,128)(2,1)S(1)} %collective-permute-done.2.w1, bf16[4,124,128]{2,1,0:T(8,128)(2,1)S(1)} %collective-permute-done.3.w2, bf16[4,124,128]{2,1,0:T(8,128)(2,1)S(1)} %collective-permute-done.4.w3), custom_call_target="tpu_custom_call" | custom-call | bytes 507904 | tf_op jit(solution)/shard_map/pallas_call | solution.py:410
  28.9 8.2 %all-to-all-start = ((bf16[8,124,128]{2,1,0:T(8,128)(2,1)}), bf16[8,124,128]{2,1,0:T(8,128)(2,1)S(1)}, u32[]{:S(2)}, u32[]{:S(2)}) async-start(bf16[8,124,128]{2,1,0:T(8,128)(2,1)} %get-tuple-element.50), calls=%async_computation | async-start | bytes 524288 | tf_op jit(solution)/shard_map/all_to_all | solution.py:465
  37.4 3.0 %collective-permute-start.6 = (bf16[2,320,128]{2,1,0:T(8,128)(2,1)S(1)}, bf16[2,320,128]{2,1,0:T(8,128)(2,1)S(1)}, u32[]{:S(2)}, u32[]{:S(2)}) collective-permute-start(bf16[2,320,128]{2,1,0:T(8,128)(2,1)S(1)} %get-tuple-element.45), channel_id=1, source_target_pairs={{0,2},{2,0},{1,3},{3,1},{4,6},{6,4},{5,7},{7,5},{8,10},{10,8},{9,1... | collective-permute-start | bytes 491528 | tf_op jit(solution)/shard_map/ppermute | solution.py:473
  42.8 3.7 %all-to-all-done.w0 = bf16[8,124,128]{2,1,0:T(8,128)(2,1)S(1)} async-done(((bf16[8,124,128]{2,1,0:T(8,128)(2,1)}), bf16[8,124,128]{2,1,0:T(8,128)(2,1)S(1)}, u32[]{:S(2)}, u32[]{:S(2)}) %all-to-all-start) | async-done | bytes 253984 | tf_op jit(solution)/shard_map/all_to_all | solution.py:465
  47.6 2.9 %collective-permute-start.11 = (bf16[8,124,128]{2,1,0:T(8,128)(2,1)S(1)}, bf16[8,124,128]{2,1,0:T(8,128)(2,1)S(1)}, u32[]{:S(2)}, u32[]{:S(2)}) collective-permute-start(bf16[8,124,128]{2,1,0:T(8,128)(2,1)S(1)} %all-to-all-done.w0), channel_id=1, source_target_pairs={{0,128},{64,192},{128,0},{192,64},{1,129},{65,193},{129,1},{193,65... | collective-permute-start | bytes 761864 | tf_op jit(solution)/shard_map/ppermute | solution.py:422
  50.5 2.1 %collective-permute-start.8 = (bf16[2,320,128]{2,1,0:T(8,128)(2,1)S(1)}, bf16[2,320,128]{2,1,0:T(8,128)(2,1)S(1)}, u32[]{:S(2)}, u32[]{:S(2)}) collective-permute-start(bf16[2,320,128]{2,1,0:T(8,128)(2,1)S(1)} %get-tuple-element.47), channel_id=1, source_target_pairs={{0,4},{1,5},{4,0},{5,1},{2,6},{3,7},{6,2},{7,3},{8,12},{9,13},{12,... | collective-permute-start | bytes 491528 | tf_op jit(solution)/shard_map/ppermute | solution.py:476
  52.5 3.7 %collective-permute-done.8.x2 = bf16[2,320,128]{2,1,0:T(8,128)(2,1)S(1)} collective-permute-done((bf16[2,320,128]{2,1,0:T(8,128)(2,1)S(1)}, bf16[2,320,128]{2,1,0:T(8,128)(2,1)S(1)}, u32[]{:S(2)}, u32[]{:S(2)}) %collective-permute-start.8) | collective-permute-done | bytes 163872 | tf_op jit(solution)/shard_map/ppermute | solution.py:476
  56.2 2.1 %collective-permute-done.9.x3 = bf16[2,320,128]{2,1,0:T(8,128)(2,1)S(1)} collective-permute-done((bf16[2,320,128]{2,1,0:T(8,128)(2,1)S(1)}, bf16[2,320,128]{2,1,0:T(8,128)(2,1)S(1)}, u32[]{:S(2)}, u32[]{:S(2)}) %collective-permute-start.9) | collective-permute-done | bytes 163872 | tf_op jit(solution)/shard_map/ppermute | solution.py:476
  59.6 5.4 %shard_map.99 = (bf16[4,14,48,128]{3,2,1,0:T(8,128)(2,1)S(1)}, bf16[4,14,48,128]{3,2,1,0:T(8,128)(2,1)S(1)}) custom-call(bf16[3,36,80,128]{3,2,1,0:T(8,128)(2,1)S(1)} %get-tuple-element.48.even, bf16[3,36,64,128]{3,2,1,0:T(8,128)(2,1)S(1)} %get-tuple-element.49.odd, bf16[8,124,128]{2,1,0:T(8,128)(2,1)S(1)} %all-to-all-done.w0, ...), custom_call_target="tpu_custom_call" | custom-call | flops 3850371072 | bytes 4997120 | tf_op jit(solution)/shard_map/pallas_call | solution.py:410
  65.1 5.2 %collective-permute-start.13 = (bf16[4,14,48,128]{3,2,1,0:T(8,128)(2,1)S(1)}, bf16[4,14,48,128]{3,2,1,0:T(8,128)(2,1)S(1)}, u32[]{:S(2)}, u32[]{:S(2)}) collective-permute-start(bf16[4,14,48,128]{3,2,1,0:T(8,128)(2,1)S(1)} %get-tuple-element.52), channel_id=1, source_target_pairs={{0,2},{2,0},{1,3},{3,1},{4,6},{6,4},{5,7},{7,5},{8,10},{10,8},{9,1... | collective-permute-start | bytes 2064392 | tf_op jit(solution)/shard_map/ppermute | solution.py:499
  70.3 1.8 %collective-permute-done.13.y = bf16[4,14,48,128]{3,2,1,0:T(8,128)(2,1)S(1)} collective-permute-done((bf16[4,14,48,128]{3,2,1,0:T(8,128)(2,1)S(1)}, bf16[4,14,48,128]{3,2,1,0:T(8,128)(2,1)S(1)}, u32[]{:S(2)}, u32[]{:S(2)}) %collective-permute-start.13) | collective-permute-done | bytes 688160 | tf_op jit(solution)/shard_map/ppermute | solution.py:499
  73.0 1.9 %collective-permute-start.15 = (bf16[14,48,128]{2,1,0:T(8,128)(2,1)S(1)}, bf16[14,48,128]{2,1,0:T(8,128)(2,1)S(1)}, u32[]{:S(2)}, u32[]{:S(2)}) collective-permute-start(bf16[14,48,128]{2,1,0:T(8,128)(2,1)S(1)} %get-tuple-element.55), channel_id=1, source_target_pairs={{0,4},{1,5},{4,0},{5,1},{2,6},{3,7},{6,2},{7,3},{8,12},{9,13},{12,... | collective-permute-start | bytes 516104 | tf_op jit(solution)/shard_map/ppermute | solution.py:502
  74.9 1.4 %collective-permute-start.16 = (bf16[14,48,128]{2,1,0:T(8,128)(2,1)S(1)}, bf16[14,48,128]{2,1,0:T(8,128)(2,1)S(1)}, u32[]{:S(2)}, u32[]{:S(2)}) collective-permute-start(bf16[14,48,128]{2,1,0:T(8,128)(2,1)S(1)} %get-tuple-element.56), channel_id=1, source_target_pairs={{0,5},{1,4},{4,1},{5,0},{2,7},{3,6},{6,3},{7,2},{8,13},{9,12},{12,... | collective-permute-start | bytes 516104 | tf_op jit(solution)/shard_map/ppermute | solution.py:502
  76.3 1.8 %collective-permute-done.14.x1 = bf16[14,48,128]{2,1,0:T(8,128)(2,1)S(1)} collective-permute-done((bf16[14,48,128]{2,1,0:T(8,128)(2,1)S(1)}, bf16[14,48,128]{2,1,0:T(8,128)(2,1)S(1)}, u32[]{:S(2)}, u32[]{:S(2)}) %collective-permute-start.14) | collective-permute-done | bytes 172064 | tf_op jit(solution)/shard_map/ppermute | solution.py:502
  78.2 4.6 %collective-permute-done.15.x2 = bf16[14,48,128]{2,1,0:T(8,128)(2,1)S(1)} collective-permute-done((bf16[14,48,128]{2,1,0:T(8,128)(2,1)S(1)}, bf16[14,48,128]{2,1,0:T(8,128)(2,1)S(1)}, u32[]{:S(2)}, u32[]{:S(2)}) %collective-permute-start.15) | collective-permute-done | bytes 172064 | tf_op jit(solution)/shard_map/ppermute | solution.py:502
  82.8 2.7 %collective-permute-done.16.x3 = bf16[14,48,128]{2,1,0:T(8,128)(2,1)S(1)} collective-permute-done((bf16[14,48,128]{2,1,0:T(8,128)(2,1)S(1)}, bf16[14,48,128]{2,1,0:T(8,128)(2,1)S(1)}, u32[]{:S(2)}, u32[]{:S(2)}) %collective-permute-start.16) | collective-permute-done | bytes 172064 | tf_op jit(solution)/shard_map/ppermute | solution.py:502
  87.2 1.3 %collective-permute-done.17.other = bf16[9,48,384]{2,1,0:T(8,128)(2,1)S(1)} collective-permute-done((bf16[9,48,384]{2,1,0:T(8,128)(2,1)S(1)}, bf16[9,48,384]{2,1,0:T(8,128)(2,1)S(1)}, u32[]{:S(2)}, u32[]{:S(2)}) %collective-permute-start.17) | collective-permute-done | bytes 331808 | tf_op jit(solution)/shard_map/ppermute | solution.py:505
  88.5 2.1 %copy-done.6 = bf16[992,16,128]{2,1,0:T(8,128)(2,1)S(1)} copy-done((bf16[992,16,128]{2,1,0:T(8,128)(2,1)S(1)}, bf16[992,16,128]{2,1,0:T(8,128)(2,1)}, u32[]{:S(2)}) %copy-start.6) | copy-done | bytes 4063256
  90.6 3.6 %shard_map.102 = (f32[256,256]{1,0:T(8,128)S(1)}, f32[256,256]{1,0:T(8,128)S(1)}) custom-call(bf16[9,48,384]{2,1,0:T(8,128)(2,1)S(1)} %shard_map.101.mine, bf16[9,48,384]{2,1,0:T(8,128)(2,1)S(1)} %collective-permute-done.17.other, bf16[8,124,16,128]{3,2,1,0:T(8,128)(2,1)S(1)} %bitcast.8, f32[384]{0:T(512)S(1)} %copy-done.7), custom_call_target="tpu_custom_call" | custom-call | flops 2717908992 | bytes 4728320 | tf_op jit(solution)/shard_map/pallas_call | solution.py:410
  (48 shorter events, 16.5 us)
Async XLA Ops:
  6.5 30.5 %copy-start.5 = (f32[384]{0:T(512)S(1)}, f32[384]{0:T(512)}, u32[]{:S(2)}) copy-start(f32[384]{0:T(512)} %gain.1) | copy-start | bytes 4612
  6.5 81.9 %all-gather.3.cloned.1.call-start = ((), (), s32[]{:S(2)}) async-start(), calls=%async_computation.1 | async-start | bytes 4571136 | tf_op jit(solution)/shard_map/all_gather | solution.py:466
  8.4 4.3 %collective-permute-start = (bf16[124,128]{1,0:T(8,128)(2,1)}, bf16[124,128]{1,0:T(8,128)(2,1)S(1)}, u32[]{:S(2)}, u32[]{:S(2)}) collective-permute-start(bf16[124,128]{1,0:T(8,128)(2,1)} %get-tuple-element.35), channel_id=1, source_target_pairs={{0,2},{2,0},{1,3},{3,1},{4,6},{6,4},{5,7},{7,5},{8,10},{10,8},{9,1... | collective-permute-start | bytes 95240 | tf_op jit(solution)/shard_map/ppermute | solution.py:438
  13.5 4.7 %collective-permute-start.1 = (bf16[2,124,128]{2,1,0:T(8,128)(2,1)S(1)}, bf16[2,124,128]{2,1,0:T(8,128)(2,1)S(1)}, u32[]{:S(2)}, u32[]{:S(2)}) collective-permute-start(bf16[2,124,128]{2,1,0:T(8,128)(2,1)S(1)} %shard_map.92.mine), channel_id=1, source_target_pairs={{0,4},{4,0},{1,5},{5,1},{2,6},{6,2},{3,7},{7,3},{8,12},{12,8},{9,1... | collective-permute-start | bytes 190472 | tf_op jit(solution)/shard_map/ppermute | solution.py:457
  18.2 8.3 %collective-permute-start.2 = (bf16[4,124,128]{2,1,0:T(8,128)(2,1)S(1)}, bf16[4,124,128]{2,1,0:T(8,128)(2,1)S(1)}, u32[]{:S(2)}, u32[]{:S(2)}) collective-permute-start(bf16[4,124,128]{2,1,0:T(8,128)(2,1)S(1)} %bitcast.4), channel_id=1, source_target_pairs={{0,64},{64,128},{128,192},{192,0},{1,65},{65,129},{129,193},{193,1... | collective-permute-start | bytes 380936 | tf_op jit(solution)/shard_map/ppermute | solution.py:422
  18.8 8.4 %collective-permute-start.3 = (bf16[4,124,128]{2,1,0:T(8,128)(2,1)S(1)}, bf16[4,124,128]{2,1,0:T(8,128)(2,1)S(1)}, u32[]{:S(2)}, u32[]{:S(2)}) collective-permute-start(bf16[4,124,128]{2,1,0:T(8,128)(2,1)S(1)} %bitcast.5), channel_id=1, source_target_pairs={{0,128},{64,192},{128,0},{192,64},{1,129},{65,193},{129,1},{193,65... | collective-permute-start | bytes 380936 | tf_op jit(solution)/shard_map/ppermute | solution.py:422
  21.4 5.8 %collective-permute-start.4 = (bf16[4,124,128]{2,1,0:T(8,128)(2,1)S(1)}, bf16[4,124,128]{2,1,0:T(8,128)(2,1)S(1)}, u32[]{:S(2)}, u32[]{:S(2)}) collective-permute-start(bf16[4,124,128]{2,1,0:T(8,128)(2,1)S(1)} %bitcast.6), channel_id=1, source_target_pairs={{0,192},{64,0},{128,64},{192,128},{1,193},{65,1},{129,65},{193,129... | collective-permute-start | bytes 380936 | tf_op jit(solution)/shard_map/ppermute | solution.py:422
  22.5 6.4 %collective-permute-start.5 = (bf16[96,384]{1,0:T(8,128)(2,1)}, bf16[96,384]{1,0:T(8,128)(2,1)S(1)}, u32[]{:S(2)}, u32[]{:S(2)}) collective-permute-start(bf16[96,384]{1,0:T(8,128)(2,1)} %get-tuple-element.42), channel_id=1, source_target_pairs={{0,254},{2,4},{4,2},{6,8},{8,6},{10,12},{12,10},{14,16},{16,14},{1... | collective-permute-start | bytes 221192 | tf_op jit(solution)/shard_map/ppermute | solution.py:462
  28.9 17.6 %all-to-all-start = ((bf16[8,124,128]{2,1,0:T(8,128)(2,1)}), bf16[8,124,128]{2,1,0:T(8,128)(2,1)S(1)}, u32[]{:S(2)}, u32[]{:S(2)}) async-start(bf16[8,124,128]{2,1,0:T(8,128)(2,1)} %get-tuple-element.50), calls=%async_computation | async-start | bytes 524288 | tf_op jit(solution)/shard_map/all_to_all | solution.py:465
  37.4 4.1 %collective-permute-start.6 = (bf16[2,320,128]{2,1,0:T(8,128)(2,1)S(1)}, bf16[2,320,128]{2,1,0:T(8,128)(2,1)S(1)}, u32[]{:S(2)}, u32[]{:S(2)}) collective-permute-start(bf16[2,320,128]{2,1,0:T(8,128)(2,1)S(1)} %get-tuple-element.45), channel_id=1, source_target_pairs={{0,2},{2,0},{1,3},{3,1},{4,6},{6,4},{5,7},{7,5},{8,10},{10,8},{9,1... | collective-permute-start | bytes 491528 | tf_op jit(solution)/shard_map/ppermute | solution.py:473
  41.5 11.0 %collective-permute-start.7 = (bf16[2,320,128]{2,1,0:T(8,128)(2,1)S(1)}, bf16[2,320,128]{2,1,0:T(8,128)(2,1)S(1)}, u32[]{:S(2)}, u32[]{:S(2)}) collective-permute-start(bf16[2,320,128]{2,1,0:T(8,128)(2,1)S(1)} %get-tuple-element.46.x0), channel_id=1, source_target_pairs={{0,1},{1,0},{4,5},{5,4},{2,3},{3,2},{6,7},{7,6},{8,9},{9,8},{12,13... | collective-permute-start | bytes 491528 | tf_op jit(solution)/shard_map/ppermute | solution.py:476
  46.5 13.1 %collective-permute-start.10 = (bf16[8,124,128]{2,1,0:T(8,128)(2,1)S(1)}, bf16[8,124,128]{2,1,0:T(8,128)(2,1)S(1)}, u32[]{:S(2)}, u32[]{:S(2)}) collective-permute-start(bf16[8,124,128]{2,1,0:T(8,128)(2,1)S(1)} %all-to-all-done.w0), channel_id=1, source_target_pairs={{0,64},{64,128},{128,192},{192,0},{1,65},{65,129},{129,193},{193,1... | collective-permute-start | bytes 761864 | tf_op jit(solution)/shard_map/ppermute | solution.py:422
  47.6 12.0 %collective-permute-start.11 = (bf16[8,124,128]{2,1,0:T(8,128)(2,1)S(1)}, bf16[8,124,128]{2,1,0:T(8,128)(2,1)S(1)}, u32[]{:S(2)}, u32[]{:S(2)}) collective-permute-start(bf16[8,124,128]{2,1,0:T(8,128)(2,1)S(1)} %all-to-all-done.w0), channel_id=1, source_target_pairs={{0,128},{64,192},{128,0},{192,64},{1,129},{65,193},{129,1},{193,65... | collective-permute-start | bytes 761864 | tf_op jit(solution)/shard_map/ppermute | solution.py:422
  50.5 9.1 %collective-permute-start.12 = (bf16[8,124,128]{2,1,0:T(8,128)(2,1)S(1)}, bf16[8,124,128]{2,1,0:T(8,128)(2,1)S(1)}, u32[]{:S(2)}, u32[]{:S(2)}) collective-permute-start(bf16[8,124,128]{2,1,0:T(8,128)(2,1)S(1)} %all-to-all-done.w0), channel_id=1, source_target_pairs={{0,192},{64,0},{128,64},{192,128},{1,193},{65,1},{129,65},{193,129... | collective-permute-start | bytes 761864 | tf_op jit(solution)/shard_map/ppermute | solution.py:422
  50.5 5.7 %collective-permute-start.8 = (bf16[2,320,128]{2,1,0:T(8,128)(2,1)S(1)}, bf16[2,320,128]{2,1,0:T(8,128)(2,1)S(1)}, u32[]{:S(2)}, u32[]{:S(2)}) collective-permute-start(bf16[2,320,128]{2,1,0:T(8,128)(2,1)S(1)} %get-tuple-element.47), channel_id=1, source_target_pairs={{0,4},{1,5},{4,0},{5,1},{2,6},{3,7},{6,2},{7,3},{8,12},{9,13},{12,... | collective-permute-start | bytes 491528 | tf_op jit(solution)/shard_map/ppermute | solution.py:476
  52.5 5.8 %collective-permute-start.9 = (bf16[2,320,128]{2,1,0:T(8,128)(2,1)S(1)}, bf16[2,320,128]{2,1,0:T(8,128)(2,1)S(1)}, u32[]{:S(2)}, u32[]{:S(2)}) collective-permute-start(bf16[2,320,128]{2,1,0:T(8,128)(2,1)S(1)} %get-tuple-element.47), channel_id=1, source_target_pairs={{0,5},{1,4},{4,1},{5,0},{2,7},{3,6},{6,3},{7,2},{8,13},{9,12},{12,... | collective-permute-start | bytes 491528 | tf_op jit(solution)/shard_map/ppermute | solution.py:476
  59.6 25.9 %copy-start.2 = (bf16[8,16,384]{2,1,0:T(8,128)(2,1)S(1)}, bf16[8,16,384]{2,1,0:T(8,128)(2,1)}, u32[]{:S(2)}) copy-start(bf16[8,16,384]{2,1,0:T(8,128)(2,1)} %get-tuple-element.58.cache) | copy-start | bytes 294916
  59.6 25.9 %copy-start.4 = (f32[8,384]{1,0:T(8,128)S(1)}, f32[8,384]{1,0:T(8,128)}, u32[]{:S(2)}) copy-start(f32[8,384]{1,0:T(8,128)} %get-tuple-element.57.vec) | copy-start | bytes 36868
  65.1 7.0 %collective-permute-start.13 = (bf16[4,14,48,128]{3,2,1,0:T(8,128)(2,1)S(1)}, bf16[4,14,48,128]{3,2,1,0:T(8,128)(2,1)S(1)}, u32[]{:S(2)}, u32[]{:S(2)}) collective-permute-start(bf16[4,14,48,128]{3,2,1,0:T(8,128)(2,1)S(1)} %get-tuple-element.52), channel_id=1, source_target_pairs={{0,2},{2,0},{1,3},{3,1},{4,6},{6,4},{5,7},{7,5},{8,10},{10,8},{9,1... | collective-permute-start | bytes 2064392 | tf_op jit(solution)/shard_map/ppermute | solution.py:499
  72.4 5.8 %collective-permute-start.14 = (bf16[14,48,128]{2,1,0:T(8,128)(2,1)S(1)}, bf16[14,48,128]{2,1,0:T(8,128)(2,1)S(1)}, u32[]{:S(2)}, u32[]{:S(2)}) collective-permute-start(bf16[14,48,128]{2,1,0:T(8,128)(2,1)S(1)} %get-tuple-element.54), channel_id=1, source_target_pairs={{0,1},{1,0},{4,5},{5,4},{2,3},{3,2},{6,7},{7,6},{8,9},{9,8},{12,13... | collective-permute-start | bytes 516104 | tf_op jit(solution)/shard_map/ppermute | solution.py:502
  73.0 9.8 %collective-permute-start.15 = (bf16[14,48,128]{2,1,0:T(8,128)(2,1)S(1)}, bf16[14,48,128]{2,1,0:T(8,128)(2,1)S(1)}, u32[]{:S(2)}, u32[]{:S(2)}) collective-permute-start(bf16[14,48,128]{2,1,0:T(8,128)(2,1)S(1)} %get-tuple-element.55), channel_id=1, source_target_pairs={{0,4},{1,5},{4,0},{5,1},{2,6},{3,7},{6,2},{7,3},{8,12},{9,13},{12,... | collective-permute-start | bytes 516104 | tf_op jit(solution)/shard_map/ppermute | solution.py:502
  74.9 10.5 %collective-permute-start.16 = (bf16[14,48,128]{2,1,0:T(8,128)(2,1)S(1)}, bf16[14,48,128]{2,1,0:T(8,128)(2,1)S(1)}, u32[]{:S(2)}, u32[]{:S(2)}) collective-permute-start(bf16[14,48,128]{2,1,0:T(8,128)(2,1)S(1)} %get-tuple-element.56), channel_id=1, source_target_pairs={{0,5},{1,4},{4,1},{5,0},{2,7},{3,6},{6,3},{7,2},{8,13},{9,12},{12,... | collective-permute-start | bytes 516104 | tf_op jit(solution)/shard_map/ppermute | solution.py:502
  86.0 2.5 %collective-permute-start.17 = (bf16[9,48,384]{2,1,0:T(8,128)(2,1)S(1)}, bf16[9,48,384]{2,1,0:T(8,128)(2,1)S(1)}, u32[]{:S(2)}, u32[]{:S(2)}) collective-permute-start(bf16[9,48,384]{2,1,0:T(8,128)(2,1)S(1)} %shard_map.101.mine), channel_id=1, source_target_pairs={{0,2},{2,0},{1,3},{3,1},{4,6},{6,4},{5,7},{7,5},{8,10},{10,8},{9,1... | collective-permute-start | bytes 995336 | tf_op jit(solution)/shard_map/ppermute | solution.py:505
  94.2 1.6 %collective-permute-start.18 = (f32[256,256]{1,0:T(8,128)S(1)}, f32[256,256]{1,0:T(8,128)S(1)}, u32[]{:S(2)}, u32[]{:S(2)}) collective-permute-start(f32[256,256]{1,0:T(8,128)S(1)} %get-tuple-element.62), channel_id=1, source_target_pairs={{0,2},{2,0},{1,3},{3,1},{4,6},{6,4},{5,7},{7,5},{8,10},{10,8},{9,1... | collective-permute-start | bytes 786440 | tf_op jit(solution)/shard_map/ppermute | solution.py:518
  (5 other events, 51.2 us)
Sparse Core Ops, SparseCore 0:
  29.0 57.4 all-gather.2

commit v4 on v3

--- a/solution.py
+++ b/solution.py
@@ -172,7 +172,7 @@
         out[row] = wide[pl.ds(row, 16, stride=128), :].astype(BF16)
         return carry
 
-    lax.fori_loop(0, 124, step, 0, unroll=4)
+    lax.fori_loop(0, 124, step, 0, unroll=31)
 
 
 def enter_kernel(own, gain, halo, keep, give, out_cache, edge):
@@ -234,7 +234,7 @@
             odd[p, c] = moved[1:9].reshape(64, 128).astype(BF16)
         return carry
 
-    lax.fori_loop(0, 36, spread, 0, unroll=4)
+    lax.fori_loop(0, 36, spread, 0, unroll=9)
 
 
 def first_kernel(even, odd, w0, w1, w2, w3, out_own, out_peer, wide, kernel, part_a, part_b):
@@ -350,7 +350,7 @@
                 odd[p, at] = moved[1:5].reshape(32, 384).astype(BF16)
         return carry
 
-    lax.fori_loop(0, 9, spread, 0)
+    lax.fori_loop(0, 9, spread, 0, unroll=3)
 
     def window(t):
         a, p, q = tap_of(t)

time: 104 us -> 104 us (level)
  transfers between devices with their start and end apart: 21 -> 21, of which waited for: 13 -> 14; matrix products, arithmetic and copies ran while one was open for 0% -> 0% of each run, Pallas kernels for 12% -> 12%
where the time goes in v4:
time: 104 us; the launch traced here: 103 us
  starting transfers between devices  42.3 us (41%)
  waiting for transfers between devices  26.2 us (25%)
  Pallas kernels  18.4 us (18%)
  between operations  13.5 us (13%)
  local copies, waits for them, and re-layouts  2.94 us (3%)
    pallas_call x13, Pallas kernels, run(): pl.pallas_call(kernel, out_shape=outs, in_specs=specs, out_specs=jax.tree...  18.4 us
    ppermute x3, waiting for transfers between devices, per_device(): lax.ppermute(parts[n], ('xh', 'tm'), [(i, i ^ n) for i in range(4)])  8.89 us
    all_to_all x1, starting transfers between devices, per_device(): near1 = lax.all_to_all(sent1, 'z', 0, 0)  8.2 us
    ppermute x6, starting transfers between devices, round_y(): lax.ppermute(x, 'y', [(i, (i + d) % 4) for i in range(4)])  8.13 us
    ppermute x3, waiting for transfers between devices, per_device(): lax.ppermute(v, ('xh', 'tm'), [(i, i ^ n) for i in range(4)])  5.78 us
    ppermute x1, starting transfers between devices, per_device(): part_peer = lax.ppermute(part_peer, 'core', SWAP)  5.31 us
    ppermute x1, starting transfers between devices, per_device(): lax.ppermute(edges, LON, [(i, (i + 1) % 128 if i % 2 else (i - 1) % 128)...  4.02 us
    ppermute x3, starting transfers between devices, per_device(): lax.ppermute(parts[n], ('xh', 'tm'), [(i, i ^ n) for i in range(4)])  3.95 us
  transfers between devices with their start and end apart: 21, of which 14 were waited for; matrix products, arithmetic and copies ran while one was open for 0% of the time, Pallas kernels for 12%

profile of v4, /device:TPU:1, one launch (start us, length us, event | category | flops | bytes accessed | tf_op | source)
XLA Modules:
  0.0 103.4 jit_solution(11374059383249476791)
XLA Ops:
  6.5 1.8 %shard_map.91 = (bf16[124,128]{1,0:T(8,128)(2,1)}, bf16[124,128]{1,0:T(8,128)(2,1)}, bf16[96,384]{1,0:T(8,128)(2,1)}) custom-call(bf16[3,27,384]{2,1,0:T(8,128)(2,1)} %bitcast.9, bf16[4,8,8,384]{3,2,1,0:T(8,128)(2,1)} %video.5, bf16[2,8,8,384]{3,2,1,0:T(8,128)(2,1)} %cache1.3, bf16[2,8,8,384]{3,2,1,0:T(8,128)(2,1)} %cache2.3), custom_call_target="tpu_custom_call" | custom-call | bytes 455424 | tf_op jit(solution)/shard_map/pallas_call | solution.py:410
  8.4 3.2 %collective-permute-start = (bf16[124,128]{1,0:T(8,128)(2,1)}, bf16[124,128]{1,0:T(8,128)(2,1)S(1)}, u32[]{:S(2)}, u32[]{:S(2)}) collective-permute-start(bf16[124,128]{1,0:T(8,128)(2,1)} %get-tuple-element.35), channel_id=1, source_target_pairs={{0,2},{2,0},{1,3},{3,1},{4,6},{6,4},{5,7},{7,5},{8,10},{10,8},{9,1... | collective-permute-start | bytes 95240 | tf_op jit(solution)/shard_map/ppermute | solution.py:438
  14.6 2.8 %shard_map.93 = (bf16[8,124,128]{2,1,0:T(8,128)(2,1)}, bf16[4,240,128]{2,1,0:T(8,128)(2,1)}, bf16[8,16,384]{2,1,0:T(8,128)(2,1)}, f32[8,384]{1,0:T(8,128)}) custom-call(bf16[3,27,384]{2,1,0:T(8,128)(2,1)} %bitcast.10, bf16[4,8,8,384]{3,2,1,0:T(8,128)(2,1)} %video.5, bf16[2,8,8,384]{3,2,1,0:T(8,128)(2,1)} %cache1.3, bf16[2,8,8,384]{3,2,1,0:T(8,128)(2,1)} %cache2.3, ...), custom_call_target="tpu_custom_call" | custom-call | bytes 460032 | tf_op jit(solution)/shard_map/pallas_call | solution.py:410
  18.8 2.6 %collective-permute-start.3 = (bf16[4,124,128]{2,1,0:T(8,128)(2,1)S(1)}, bf16[4,124,128]{2,1,0:T(8,128)(2,1)S(1)}, u32[]{:S(2)}, u32[]{:S(2)}) collective-permute-start(bf16[4,124,128]{2,1,0:T(8,128)(2,1)S(1)} %bitcast.5), channel_id=1, source_target_pairs={{0,128},{64,192},{128,0},{192,64},{1,129},{65,193},{129,1},{193,65... | collective-permute-start | bytes 380936 | tf_op jit(solution)/shard_map/ppermute | solution.py:422
  22.5 4.0 %collective-permute-start.5 = (bf16[96,384]{1,0:T(8,128)(2,1)}, bf16[96,384]{1,0:T(8,128)(2,1)S(1)}, u32[]{:S(2)}, u32[]{:S(2)}) collective-permute-start(bf16[96,384]{1,0:T(8,128)(2,1)} %get-tuple-element.42), channel_id=1, source_target_pairs={{0,254},{2,4},{4,2},{6,8},{8,6},{10,12},{12,10},{14,16},{16,14},{1... | collective-permute-start | bytes 221192 | tf_op jit(solution)/shard_map/ppermute | solution.py:462
  27.2 1.5 %shard_map.95 = bf16[124,16,128]{2,1,0:T(8,128)(2,1)} custom-call(bf16[4,124,128]{2,1,0:T(8,128)(2,1)S(1)} %bitcast.7, bf16[4,124,128]{2,1,0:T(8,128)(2,1)S(1)} %collective-permute-done.2.w1, bf16[4,124,128]{2,1,0:T(8,128)(2,1)S(1)} %collective-permute-done.3.w2, bf16[4,124,128]{2,1,0:T(8,128)(2,1)S(1)} %collective-permute-done.4.w3), custom_call_target="tpu_custom_call" | custom-call | bytes 507904 | tf_op jit(solution)/shard_map/pallas_call | solution.py:410
  28.8 8.2 %all-to-all-start = ((bf16[8,124,128]{2,1,0:T(8,128)(2,1)}), bf16[8,124,128]{2,1,0:T(8,128)(2,1)S(1)}, u32[]{:S(2)}, u32[]{:S(2)}) async-start(bf16[8,124,128]{2,1,0:T(8,128)(2,1)} %get-tuple-element.50), calls=%async_computation | async-start | bytes 524288 | tf_op jit(solution)/shard_map/all_to_all | solution.py:465
  37.3 3.2 %collective-permute-start.6 = (bf16[2,320,128]{2,1,0:T(8,128)(2,1)S(1)}, bf16[2,320,128]{2,1,0:T(8,128)(2,1)S(1)}, u32[]{:S(2)}, u32[]{:S(2)}) collective-permute-start(bf16[2,320,128]{2,1,0:T(8,128)(2,1)S(1)} %get-tuple-element.45), channel_id=1, source_target_pairs={{0,2},{2,0},{1,3},{3,1},{4,6},{6,4},{5,7},{7,5},{8,10},{10,8},{9,1... | collective-permute-start | bytes 491528 | tf_op jit(solution)/shard_map/ppermute | solution.py:473
  42.8 3.6 %all-to-all-done.w0 = bf16[8,124,128]{2,1,0:T(8,128)(2,1)S(1)} async-done(((bf16[8,124,128]{2,1,0:T(8,128)(2,1)}), bf16[8,124,128]{2,1,0:T(8,128)(2,1)S(1)}, u32[]{:S(2)}, u32[]{:S(2)}) %all-to-all-start) | async-done | bytes 253984 | tf_op jit(solution)/shard_map/all_to_all | solution.py:465
  47.4 2.9 %collective-permute-start.11 = (bf16[8,124,128]{2,1,0:T(8,128)(2,1)S(1)}, bf16[8,124,128]{2,1,0:T(8,128)(2,1)S(1)}, u32[]{:S(2)}, u32[]{:S(2)}) collective-permute-start(bf16[8,124,128]{2,1,0:T(8,128)(2,1)S(1)} %all-to-all-done.w0), channel_id=1, source_target_pairs={{0,128},{64,192},{128,0},{192,64},{1,129},{65,193},{129,1},{193,65... | collective-permute-start | bytes 761864 | tf_op jit(solution)/shard_map/ppermute | solution.py:422
  50.3 2.3 %collective-permute-start.8 = (bf16[2,320,128]{2,1,0:T(8,128)(2,1)S(1)}, bf16[2,320,128]{2,1,0:T(8,128)(2,1)S(1)}, u32[]{:S(2)}, u32[]{:S(2)}) collective-permute-start(bf16[2,320,128]{2,1,0:T(8,128)(2,1)S(1)} %get-tuple-element.47), channel_id=1, source_target_pairs={{0,4},{1,5},{4,0},{5,1},{2,6},{3,7},{6,2},{7,3},{8,12},{9,13},{12,... | collective-permute-start | bytes 491528 | tf_op jit(solution)/shard_map/ppermute | solution.py:476
  52.6 3.4 %collective-permute-done.8.x2 = bf16[2,320,128]{2,1,0:T(8,128)(2,1)S(1)} collective-permute-done((bf16[2,320,128]{2,1,0:T(8,128)(2,1)S(1)}, bf16[2,320,128]{2,1,0:T(8,128)(2,1)S(1)}, u32[]{:S(2)}, u32[]{:S(2)}) %collective-permute-start.8) | collective-permute-done | bytes 163872 | tf_op jit(solution)/shard_map/ppermute | solution.py:476
  56.0 2.4 %collective-permute-done.9.x3 = bf16[2,320,128]{2,1,0:T(8,128)(2,1)S(1)} collective-permute-done((bf16[2,320,128]{2,1,0:T(8,128)(2,1)S(1)}, bf16[2,320,128]{2,1,0:T(8,128)(2,1)S(1)}, u32[]{:S(2)}, u32[]{:S(2)}) %collective-permute-start.9) | collective-permute-done | bytes 163872 | tf_op jit(solution)/shard_map/ppermute | solution.py:476
  59.6 5.4 %shard_map.99 = (bf16[4,14,48,128]{3,2,1,0:T(8,128)(2,1)S(1)}, bf16[4,14,48,128]{3,2,1,0:T(8,128)(2,1)S(1)}) custom-call(bf16[3,36,80,128]{3,2,1,0:T(8,128)(2,1)S(1)} %get-tuple-element.48.even, bf16[3,36,64,128]{3,2,1,0:T(8,128)(2,1)S(1)} %get-tuple-element.49.odd, bf16[8,124,128]{2,1,0:T(8,128)(2,1)S(1)} %all-to-all-done.w0, ...), custom_call_target="tpu_custom_call" | custom-call | flops 3850371072 | bytes 4997120 | tf_op jit(solution)/shard_map/pallas_call | solution.py:410
  65.1 5.3 %collective-permute-start.13 = (bf16[4,14,48,128]{3,2,1,0:T(8,128)(2,1)S(1)}, bf16[4,14,48,128]{3,2,1,0:T(8,128)(2,1)S(1)}, u32[]{:S(2)}, u32[]{:S(2)}) collective-permute-start(bf16[4,14,48,128]{3,2,1,0:T(8,128)(2,1)S(1)} %get-tuple-element.52), channel_id=1, source_target_pairs={{0,2},{2,0},{1,3},{3,1},{4,6},{6,4},{5,7},{7,5},{8,10},{10,8},{9,1... | collective-permute-start | bytes 2064392 | tf_op jit(solution)/shard_map/ppermute | solution.py:499
  70.4 1.8 %collective-permute-done.13.y = bf16[4,14,48,128]{3,2,1,0:T(8,128)(2,1)S(1)} collective-permute-done((bf16[4,14,48,128]{3,2,1,0:T(8,128)(2,1)S(1)}, bf16[4,14,48,128]{3,2,1,0:T(8,128)(2,1)S(1)}, u32[]{:S(2)}, u32[]{:S(2)}) %collective-permute-start.13) | collective-permute-done | bytes 688160 | tf_op jit(solution)/shard_map/ppermute | solution.py:499
  72.9 1.9 %collective-permute-start.15 = (bf16[14,48,128]{2,1,0:T(8,128)(2,1)S(1)}, bf16[14,48,128]{2,1,0:T(8,128)(2,1)S(1)}, u32[]{:S(2)}, u32[]{:S(2)}) collective-permute-start(bf16[14,48,128]{2,1,0:T(8,128)(2,1)S(1)} %get-tuple-element.55), channel_id=1, source_target_pairs={{0,4},{1,5},{4,0},{5,1},{2,6},{3,7},{6,2},{7,3},{8,12},{9,13},{12,... | collective-permute-start | bytes 516104 | tf_op jit(solution)/shard_map/ppermute | solution.py:502
  74.8 1.6 %collective-permute-start.16 = (bf16[14,48,128]{2,1,0:T(8,128)(2,1)S(1)}, bf16[14,48,128]{2,1,0:T(8,128)(2,1)S(1)}, u32[]{:S(2)}, u32[]{:S(2)}) collective-permute-start(bf16[14,48,128]{2,1,0:T(8,128)(2,1)S(1)} %get-tuple-element.56), channel_id=1, source_target_pairs={{0,5},{1,4},{4,1},{5,0},{2,7},{3,6},{6,3},{7,2},{8,13},{9,12},{12,... | collective-permute-start | bytes 516104 | tf_op jit(solution)/shard_map/ppermute | solution.py:502
  76.4 1.8 %collective-permute-done.14.x1 = bf16[14,48,128]{2,1,0:T(8,128)(2,1)S(1)} collective-permute-done((bf16[14,48,128]{2,1,0:T(8,128)(2,1)S(1)}, bf16[14,48,128]{2,1,0:T(8,128)(2,1)S(1)}, u32[]{:S(2)}, u32[]{:S(2)}) %collective-permute-start.14) | collective-permute-done | bytes 172064 | tf_op jit(solution)/shard_map/ppermute | solution.py:502
  78.3 4.4 %collective-permute-done.15.x2 = bf16[14,48,128]{2,1,0:T(8,128)(2,1)S(1)} collective-permute-done((bf16[14,48,128]{2,1,0:T(8,128)(2,1)S(1)}, bf16[14,48,128]{2,1,0:T(8,128)(2,1)S(1)}, u32[]{:S(2)}, u32[]{:S(2)}) %collective-permute-start.15) | collective-permute-done | bytes 172064 | tf_op jit(solution)/shard_map/ppermute | solution.py:502
  82.7 2.7 %collective-permute-done.16.x3 = bf16[14,48,128]{2,1,0:T(8,128)(2,1)S(1)} collective-permute-done((bf16[14,48,128]{2,1,0:T(8,128)(2,1)S(1)}, bf16[14,48,128]{2,1,0:T(8,128)(2,1)S(1)}, u32[]{:S(2)}, u32[]{:S(2)}) %collective-permute-start.16) | collective-permute-done | bytes 172064 | tf_op jit(solution)/shard_map/ppermute | solution.py:502
  87.1 1.3 %collective-permute-done.17.other = bf16[9,48,384]{2,1,0:T(8,128)(2,1)S(1)} collective-permute-done((bf16[9,48,384]{2,1,0:T(8,128)(2,1)S(1)}, bf16[9,48,384]{2,1,0:T(8,128)(2,1)S(1)}, u32[]{:S(2)}, u32[]{:S(2)}) %collective-permute-start.17) | collective-permute-done | bytes 331808 | tf_op jit(solution)/shard_map/ppermute | solution.py:505
  88.3 2.1 %copy-done.6 = bf16[992,16,128]{2,1,0:T(8,128)(2,1)S(1)} copy-done((bf16[992,16,128]{2,1,0:T(8,128)(2,1)S(1)}, bf16[992,16,128]{2,1,0:T(8,128)(2,1)}, u32[]{:S(2)}) %copy-start.6) | copy-done | bytes 4063256
  90.5 3.4 %shard_map.102 = (f32[256,256]{1,0:T(8,128)S(1)}, f32[256,256]{1,0:T(8,128)S(1)}) custom-call(bf16[9,48,384]{2,1,0:T(8,128)(2,1)S(1)} %shard_map.101.mine, bf16[9,48,384]{2,1,0:T(8,128)(2,1)S(1)} %collective-permute-done.17.other, bf16[8,124,16,128]{3,2,1,0:T(8,128)(2,1)S(1)} %bitcast.8, f32[384]{0:T(512)S(1)} %copy-done.7), custom_call_target="tpu_custom_call" | custom-call | flops 2717908992 | bytes 4728320 | tf_op jit(solution)/shard_map/pallas_call | solution.py:410
  (48 shorter events, 16.1 us)
Async XLA Ops:
  6.5 30.4 %copy-start.5 = (f32[384]{0:T(512)S(1)}, f32[384]{0:T(512)}, u32[]{:S(2)}) copy-start(f32[384]{0:T(512)} %gain.1) | copy-start | bytes 4612
  6.5 81.8 %all-gather.3.cloned.1.call-start = ((), (), s32[]{:S(2)}) async-start(), calls=%async_computation.1 | async-start | bytes 4571136 | tf_op jit(solution)/shard_map/all_gather | solution.py:466
  8.4 4.3 %collective-permute-start = (bf16[124,128]{1,0:T(8,128)(2,1)}, bf16[124,128]{1,0:T(8,128)(2,1)S(1)}, u32[]{:S(2)}, u32[]{:S(2)}) collective-permute-start(bf16[124,128]{1,0:T(8,128)(2,1)} %get-tuple-element.35), channel_id=1, source_target_pairs={{0,2},{2,0},{1,3},{3,1},{4,6},{6,4},{5,7},{7,5},{8,10},{10,8},{9,1... | collective-permute-start | bytes 95240 | tf_op jit(solution)/shard_map/ppermute | solution.py:438
  13.5 4.7 %collective-permute-start.1 = (bf16[2,124,128]{2,1,0:T(8,128)(2,1)S(1)}, bf16[2,124,128]{2,1,0:T(8,128)(2,1)S(1)}, u32[]{:S(2)}, u32[]{:S(2)}) collective-permute-start(bf16[2,124,128]{2,1,0:T(8,128)(2,1)S(1)} %shard_map.92.mine), channel_id=1, source_target_pairs={{0,4},{4,0},{1,5},{5,1},{2,6},{6,2},{3,7},{7,3},{8,12},{12,8},{9,1... | collective-permute-start | bytes 190472 | tf_op jit(solution)/shard_map/ppermute | solution.py:457
  18.2 8.3 %collective-permute-start.2 = (bf16[4,124,128]{2,1,0:T(8,128)(2,1)S(1)}, bf16[4,124,128]{2,1,0:T(8,128)(2,1)S(1)}, u32[]{:S(2)}, u32[]{:S(2)}) collective-permute-start(bf16[4,124,128]{2,1,0:T(8,128)(2,1)S(1)} %bitcast.4), channel_id=1, source_target_pairs={{0,64},{64,128},{128,192},{192,0},{1,65},{65,129},{129,193},{193,1... | collective-permute-start | bytes 380936 | tf_op jit(solution)/shard_map/ppermute | solution.py:422
  18.8 8.4 %collective-permute-start.3 = (bf16[4,124,128]{2,1,0:T(8,128)(2,1)S(1)}, bf16[4,124,128]{2,1,0:T(8,128)(2,1)S(1)}, u32[]{:S(2)}, u32[]{:S(2)}) collective-permute-start(bf16[4,124,128]{2,1,0:T(8,128)(2,1)S(1)} %bitcast.5), channel_id=1, source_target_pairs={{0,128},{64,192},{128,0},{192,64},{1,129},{65,193},{129,1},{193,65... | collective-permute-start | bytes 380936 | tf_op jit(solution)/shard_map/ppermute | solution.py:422
  21.4 5.8 %collective-permute-start.4 = (bf16[4,124,128]{2,1,0:T(8,128)(2,1)S(1)}, bf16[4,124,128]{2,1,0:T(8,128)(2,1)S(1)}, u32[]{:S(2)}, u32[]{:S(2)}) collective-permute-start(bf16[4,124,128]{2,1,0:T(8,128)(2,1)S(1)} %bitcast.6), channel_id=1, source_target_pairs={{0,192},{64,0},{128,64},{192,128},{1,193},{65,1},{129,65},{193,129... | collective-permute-start | bytes 380936 | tf_op jit(solution)/shard_map/ppermute | solution.py:422
  22.5 6.3 %collective-permute-start.5 = (bf16[96,384]{1,0:T(8,128)(2,1)}, bf16[96,384]{1,0:T(8,128)(2,1)S(1)}, u32[]{:S(2)}, u32[]{:S(2)}) collective-permute-start(bf16[96,384]{1,0:T(8,128)(2,1)} %get-tuple-element.42), channel_id=1, source_target_pairs={{0,254},{2,4},{4,2},{6,8},{8,6},{10,12},{12,10},{14,16},{16,14},{1... | collective-permute-start | bytes 221192 | tf_op jit(solution)/shard_map/ppermute | solution.py:462
  28.8 17.6 %all-to-all-start = ((bf16[8,124,128]{2,1,0:T(8,128)(2,1)}), bf16[8,124,128]{2,1,0:T(8,128)(2,1)S(1)}, u32[]{:S(2)}, u32[]{:S(2)}) async-start(bf16[8,124,128]{2,1,0:T(8,128)(2,1)} %get-tuple-element.50), calls=%async_computation | async-start | bytes 524288 | tf_op jit(solution)/shard_map/all_to_all | solution.py:465
  37.3 4.2 %collective-permute-start.6 = (bf16[2,320,128]{2,1,0:T(8,128)(2,1)S(1)}, bf16[2,320,128]{2,1,0:T(8,128)(2,1)S(1)}, u32[]{:S(2)}, u32[]{:S(2)}) collective-permute-start(bf16[2,320,128]{2,1,0:T(8,128)(2,1)S(1)} %get-tuple-element.45), channel_id=1, source_target_pairs={{0,2},{2,0},{1,3},{3,1},{4,6},{6,4},{5,7},{7,5},{8,10},{10,8},{9,1... | collective-permute-start | bytes 491528 | tf_op jit(solution)/shard_map/ppermute | solution.py:473
  41.5 11.0 %collective-permute-start.7 = (bf16[2,320,128]{2,1,0:T(8,128)(2,1)S(1)}, bf16[2,320,128]{2,1,0:T(8,128)(2,1)S(1)}, u32[]{:S(2)}, u32[]{:S(2)}) collective-permute-start(bf16[2,320,128]{2,1,0:T(8,128)(2,1)S(1)} %get-tuple-element.46.x0), channel_id=1, source_target_pairs={{0,1},{1,0},{4,5},{5,4},{2,3},{3,2},{6,7},{7,6},{8,9},{9,8},{12,13... | collective-permute-start | bytes 491528 | tf_op jit(solution)/shard_map/ppermute | solution.py:476
  46.4 13.2 %collective-permute-start.10 = (bf16[8,124,128]{2,1,0:T(8,128)(2,1)S(1)}, bf16[8,124,128]{2,1,0:T(8,128)(2,1)S(1)}, u32[]{:S(2)}, u32[]{:S(2)}) collective-permute-start(bf16[8,124,128]{2,1,0:T(8,128)(2,1)S(1)} %all-to-all-done.w0), channel_id=1, source_target_pairs={{0,64},{64,128},{128,192},{192,0},{1,65},{65,129},{129,193},{193,1... | collective-permute-start | bytes 761864 | tf_op jit(solution)/shard_map/ppermute | solution.py:422
  47.4 12.2 %collective-permute-start.11 = (bf16[8,124,128]{2,1,0:T(8,128)(2,1)S(1)}, bf16[8,124,128]{2,1,0:T(8,128)(2,1)S(1)}, u32[]{:S(2)}, u32[]{:S(2)}) collective-permute-start(bf16[8,124,128]{2,1,0:T(8,128)(2,1)S(1)} %all-to-all-done.w0), channel_id=1, source_target_pairs={{0,128},{64,192},{128,0},{192,64},{1,129},{65,193},{129,1},{193,65... | collective-permute-start | bytes 761864 | tf_op jit(solution)/shard_map/ppermute | solution.py:422
  50.3 9.3 %collective-permute-start.12 = (bf16[8,124,128]{2,1,0:T(8,128)(2,1)S(1)}, bf16[8,124,128]{2,1,0:T(8,128)(2,1)S(1)}, u32[]{:S(2)}, u32[]{:S(2)}) collective-permute-start(bf16[8,124,128]{2,1,0:T(8,128)(2,1)S(1)} %all-to-all-done.w0), channel_id=1, source_target_pairs={{0,192},{64,0},{128,64},{192,128},{1,193},{65,1},{129,65},{193,129... | collective-permute-start | bytes 761864 | tf_op jit(solution)/shard_map/ppermute | solution.py:422
  50.3 5.7 %collective-permute-start.8 = (bf16[2,320,128]{2,1,0:T(8,128)(2,1)S(1)}, bf16[2,320,128]{2,1,0:T(8,128)(2,1)S(1)}, u32[]{:S(2)}, u32[]{:S(2)}) collective-permute-start(bf16[2,320,128]{2,1,0:T(8,128)(2,1)S(1)} %get-tuple-element.47), channel_id=1, source_target_pairs={{0,4},{1,5},{4,0},{5,1},{2,6},{3,7},{6,2},{7,3},{8,12},{9,13},{12,... | collective-permute-start | bytes 491528 | tf_op jit(solution)/shard_map/ppermute | solution.py:476
  52.6 5.8 %collective-permute-start.9 = (bf16[2,320,128]{2,1,0:T(8,128)(2,1)S(1)}, bf16[2,320,128]{2,1,0:T(8,128)(2,1)S(1)}, u32[]{:S(2)}, u32[]{:S(2)}) collective-permute-start(bf16[2,320,128]{2,1,0:T(8,128)(2,1)S(1)} %get-tuple-element.47), channel_id=1, source_target_pairs={{0,5},{1,4},{4,1},{5,0},{2,7},{3,6},{6,3},{7,2},{8,13},{9,12},{12,... | collective-permute-start | bytes 491528 | tf_op jit(solution)/shard_map/ppermute | solution.py:476
  59.6 25.7 %copy-start.2 = (bf16[8,16,384]{2,1,0:T(8,128)(2,1)S(1)}, bf16[8,16,384]{2,1,0:T(8,128)(2,1)}, u32[]{:S(2)}) copy-start(bf16[8,16,384]{2,1,0:T(8,128)(2,1)} %get-tuple-element.58.cache) | copy-start | bytes 294916
  59.6 25.7 %copy-start.4 = (f32[8,384]{1,0:T(8,128)S(1)}, f32[8,384]{1,0:T(8,128)}, u32[]{:S(2)}) copy-start(f32[8,384]{1,0:T(8,128)} %get-tuple-element.57.vec) | copy-start | bytes 36868
  65.1 7.1 %collective-permute-start.13 = (bf16[4,14,48,128]{3,2,1,0:T(8,128)(2,1)S(1)}, bf16[4,14,48,128]{3,2,1,0:T(8,128)(2,1)S(1)}, u32[]{:S(2)}, u32[]{:S(2)}) collective-permute-start(bf16[4,14,48,128]{3,2,1,0:T(8,128)(2,1)S(1)} %get-tuple-element.52), channel_id=1, source_target_pairs={{0,2},{2,0},{1,3},{3,1},{4,6},{6,4},{5,7},{7,5},{8,10},{10,8},{9,1... | collective-permute-start | bytes 2064392 | tf_op jit(solution)/shard_map/ppermute | solution.py:499
  72.5 5.8 %collective-permute-start.14 = (bf16[14,48,128]{2,1,0:T(8,128)(2,1)S(1)}, bf16[14,48,128]{2,1,0:T(8,128)(2,1)S(1)}, u32[]{:S(2)}, u32[]{:S(2)}) collective-permute-start(bf16[14,48,128]{2,1,0:T(8,128)(2,1)S(1)} %get-tuple-element.54), channel_id=1, source_target_pairs={{0,1},{1,0},{4,5},{5,4},{2,3},{3,2},{6,7},{7,6},{8,9},{9,8},{12,13... | collective-permute-start | bytes 516104 | tf_op jit(solution)/shard_map/ppermute | solution.py:502
  72.9 9.8 %collective-permute-start.15 = (bf16[14,48,128]{2,1,0:T(8,128)(2,1)S(1)}, bf16[14,48,128]{2,1,0:T(8,128)(2,1)S(1)}, u32[]{:S(2)}, u32[]{:S(2)}) collective-permute-start(bf16[14,48,128]{2,1,0:T(8,128)(2,1)S(1)} %get-tuple-element.55), channel_id=1, source_target_pairs={{0,4},{1,5},{4,0},{5,1},{2,6},{3,7},{6,2},{7,3},{8,12},{9,13},{12,... | collective-permute-start | bytes 516104 | tf_op jit(solution)/shard_map/ppermute | solution.py:502
  74.8 10.5 %collective-permute-start.16 = (bf16[14,48,128]{2,1,0:T(8,128)(2,1)S(1)}, bf16[14,48,128]{2,1,0:T(8,128)(2,1)S(1)}, u32[]{:S(2)}, u32[]{:S(2)}) collective-permute-start(bf16[14,48,128]{2,1,0:T(8,128)(2,1)S(1)} %get-tuple-element.56), channel_id=1, source_target_pairs={{0,5},{1,4},{4,1},{5,0},{2,7},{3,6},{6,3},{7,2},{8,13},{9,12},{12,... | collective-permute-start | bytes 516104 | tf_op jit(solution)/shard_map/ppermute | solution.py:502
  85.8 2.5 %collective-permute-start.17 = (bf16[9,48,384]{2,1,0:T(8,128)(2,1)S(1)}, bf16[9,48,384]{2,1,0:T(8,128)(2,1)S(1)}, u32[]{:S(2)}, u32[]{:S(2)}) collective-permute-start(bf16[9,48,384]{2,1,0:T(8,128)(2,1)S(1)} %shard_map.101.mine), channel_id=1, source_target_pairs={{0,2},{2,0},{1,3},{3,1},{4,6},{6,4},{5,7},{7,5},{8,10},{10,8},{9,1... | collective-permute-start | bytes 995336 | tf_op jit(solution)/shard_map/ppermute | solution.py:505
  93.9 1.6 %collective-permute-start.18 = (f32[256,256]{1,0:T(8,128)S(1)}, f32[256,256]{1,0:T(8,128)S(1)}, u32[]{:S(2)}, u32[]{:S(2)}) collective-permute-start(f32[256,256]{1,0:T(8,128)S(1)} %get-tuple-element.62), channel_id=1, source_target_pairs={{0,2},{2,0},{1,3},{3,1},{4,6},{6,4},{5,7},{7,5},{8,10},{10,8},{9,1... | collective-permute-start | bytes 786440 | tf_op jit(solution)/shard_map/ppermute | solution.py:518
  (5 other events, 50.8 us)
Sparse Core Ops, SparseCore 0:
  28.9 57.5 all-gather.2
